TPU v7x, 32 devices: a whole 2x2x4 slice. The times are simulated.
32 devices in a mesh: tok: 4 (over y, x), chan: 8 (over z, core).
Axes of the slice: x: 2, y: 2, z: 4, core: 2. Of those that a mesh axis runs over, the one named last changes fastest.
Arguments:
- acts: bfloat16 [2048, 28672], P('tok', 'chan'), may hold values from -6 to 6
- target: bfloat16 [2048, 8192], P('tok', 'chan'), may hold values from -6 to 6
- proj_b: bfloat16 [2048, 28672], P(None, 'chan'), may hold values from -0.03125 to 0.03125
- proj_a: bfloat16 [8192, 2048], P('chan'), may hold values from -0.125 to 0.125
Outputs:
- grad_a: float32 [8192, 2048], P('chan', 'tok')
- grad_b: float32 [2048, 28672], P('tok', 'chan')
All inputs are finite; a program needn't handle non-finite values.
Results may differ from a plain program's by a relative error of at most 0.004.
Values may be sent and summed in bfloat16 or wider, within the bound.
A program may use at most 192 MiB of HBM per device.

v0:
```python
import jax
import jax.numpy as jnp
from jax import lax
from jax.sharding import PartitionSpec as P


def contract_rows(left, right):
    return lax.dot_general(
        left, right, (((0,), (0,)), ((), ())), preferred_element_type=jnp.float32
    )


def local(acts, target, proj_b, proj_a):
    partial_value = lax.dot_general(
        acts, proj_b, (((1,), (1,)), ((), ())), preferred_element_type=jnp.float32
    )
    codes = lax.psum(partial_value, "chan").astype(jnp.bfloat16)
    predicted = lax.dot_general(
        codes, proj_a, (((1,), (1,)), ((), ())), preferred_element_type=jnp.float32
    )
    residual = (target.astype(jnp.float32) - predicted).astype(jnp.bfloat16)
    grad_partial = jnp.dot(residual, proj_a, preferred_element_type=jnp.float32)
    grad_codes = lax.psum(grad_partial, "chan").astype(jnp.bfloat16)
    factor_scale = -2.0 / (acts.shape[0] * lax.axis_size("tok"))
    term_a = contract_rows(residual, codes)
    grad_a = lax.psum_scatter(term_a, "tok", scatter_dimension=1, tiled=True) * factor_scale
    grad_b = (
        lax.psum_scatter(contract_rows(grad_codes, acts), "tok", scatter_dimension=0, tiled=True)
        * factor_scale
    )
    return (grad_a, grad_b)


def solution(mesh):
    return jax.shard_map(
        local,
        mesh=mesh,
        in_specs=(P("tok", "chan"), P("tok", "chan"), P(None, "chan"), P("chan", None)),
        out_specs=(P("chan", "tok"), P("tok", "chan")),
        check_vma=False,
    )
```

profile of v0, /device:TPU:0, one launch (start us, length us, event | category | flops | bytes accessed | tf_op | source)
XLA Modules:
  0.0 503.2 jit_solution(3370395371150071835)
XLA Ops:
  7.2 0.0 reduce-scatter.3.cloned.1.call-start
  7.2 13.4 %fusion.9 = f32[512,2048]{1,0:T(8,128)} fusion(bf16[512,3584]{1,0:T(8,128)(2,1)} %param.4, bf16[2048,3584]{1,0:T(8,128)(2,1)} %param.6), kind=kOutput, calls=%fused_computation.12 | convolution fusion | flops 7516192768 | bytes 22544384 | tf_op jit(solution)/shard_map/dot_general | solution.py:14
  20.6 90.8 %all-reduce.2 = bf16[512,2048]{1,0:T(8,128)(2,1)S(1)} all-reduce(f32[512,2048]{1,0:T(8,128)} %fusion.9), channel_id=1, replica_groups=mesh['tok'=4,'chan'=8] {'chan'}, use_global_device_ids=true, to_apply=%region_0.0 | all-reduce | flops 1048576 | bytes 6291456 | tf_op jit(solution)/shard_map/psum | solution.py:17
  111.5 0.0 copy-start.2
  111.5 4.6 fusion.11
  116.1 0.0 copy-start
  116.1 1.3 copy-done
  117.4 0.0 copy-done.2
  117.4 5.7 %fusion.3 = f32[1024,2048]{1,0:T(8,128)} fusion(f32[512,1024]{1,0:T(8,128)S(1)} %fusion.11, bf16[512,1024]{1,0:T(8,128)(2,1)S(1)} %copy-done.2, bf16[512,2048]{1,0:T(8,128)(2,1)S(1)} %all-reduce.2), kind=kOutput, calls=%fused_computation.5 | convolution fusion | flops 2149056512 | bytes 13631488 | tf_op jit(solution)/shard_map/dot_general | solution.py:8
  123.2 0.0 copy-start.1
  123.2 0.0 reduce-scatter.3.cloned.1.call-update
  123.2 0.0 reduce-scatter.5.cloned.1.call-start
  123.3 1.5 copy-done.1
  124.8 6.5 %fusion.2 = f32[512,2048]{1,0:T(8,128)} fusion(bf16[1024,2048]{1,0:T(8,128)(2,1)} %param.7, f32[512,1024]{1,0:T(8,128)S(1)} %copy-done.1, bf16[512,1024]{1,0:T(8,128)(2,1)S(1)} %copy-done.2), kind=kOutput, calls=%fused_computation.4 | convolution fusion | flops 2149056512 | bytes 11534336 | tf_op jit(solution)/shard_map/dot_general | solution.py:22
  131.3 87.6 %all-reduce.3 = bf16[512,2048]{1,0:T(8,128)(2,1)S(1)} all-reduce(f32[512,2048]{1,0:T(8,128)} %fusion.2), channel_id=1, replica_groups=mesh['tok'=4,'chan'=8] {'chan'}, use_global_device_ids=true, to_apply=%region_2.0 | all-reduce | flops 1048576 | bytes 6291456 | tf_op jit(solution)/shard_map/psum | solution.py:23
  218.9 15.7 %fusion.10 = f32[2048,3584]{1,0:T(8,128)} fusion(bf16[512,2048]{1,0:T(8,128)(2,1)S(1)} %all-reduce.3, bf16[512,3584]{1,0:T(8,128)(2,1)} %param.4), kind=kOutput, calls=%fused_computation.13 | convolution fusion | flops 7516192768 | bytes 35127296 | tf_op jit(solution)/shard_map/dot_general | solution.py:8
  234.6 0.0 reduce-scatter.5.cloned.1.call-update
  234.6 0.0 reduce-scatter.3.cloned.1.call-done
  234.6 3.1 broadcast_multiply_fusion.1
  237.8 251.9 %reduce-scatter.5.cloned.1.call-done = f32[512,3584]{1,0:T(8,128)} async-done(((f32[2048,3584]{1,0:T(8,128)}), f32[512,3584]{1,0:T(8,128)}) %reduce-scatter.5.cloned.1.call-update) | async-done | bytes 7340048 | tf_op jit(solution)/shard_map/reduce_scatter | solution.py:28
  489.7 6.7 %broadcast_multiply_fusion = f32[512,3584]{1,0:T(8,128)} fusion(f32[512,3584]{1,0:T(8,128)} %reduce-scatter.5.cloned.1.call-done), kind=kLoop, calls=%fused_computation | loop fusion | flops 1835008 | bytes 14680064 | tf_op jit(solution)/shard_map/mul | solution.py:28
Async XLA Ops:
  7.2 227.5 %reduce-scatter.3.cloned.1.call-start = ((), (), s32[]{:S(2)}) async-start(), calls=%async_computation.2 | async-start | bytes 10485760 | tf_op jit(solution)/shard_map/reduce_scatter | solution.py:26
  111.5 6.0 %copy-start.2 = (bf16[512,1024]{1,0:T(8,128)(2,1)S(1)}, bf16[512,1024]{1,0:T(8,128)(2,1)}, u32[]{:S(2)}) copy-start(bf16[512,1024]{1,0:T(8,128)(2,1)} %param.5) | copy-start | bytes 3145732
  116.1 1.3 copy-start
  123.2 1.6 copy-start.1
  123.2 366.5 %reduce-scatter.5.cloned.1.call-start = ((), (), s32[]{:S(2)}) async-start(), calls=%async_computation.3 | async-start | bytes 36700160 | tf_op jit(solution)/shard_map/reduce_scatter | solution.py:28
Sparse Core Ops, SparseCore 0:
  123.3 85.6 reduce-scatter.2
  234.7 254.9 reduce-scatter.4
where the time goes:
time: 504 us; the launch traced here: 503 us
  waiting for transfers between devices  252 us (50%)
  blocking collectives  178 us (35%)
  matrix products  46 us (9%)
  between operations  14.1 us (3%)
  other arithmetic  9.86 us (2%)
    reduce_scatter x1, waiting for transfers between devices, local(): lax.psum_scatter(contract_rows(grad_codes, acts), 'tok', scatter_dimensio...  252 us
    psum x1, blocking collectives, local(): codes = lax.psum(partial_value, 'chan').astype(jnp.bfloat16)  90.8 us
    psum x1, blocking collectives, local(): grad_codes = lax.psum(grad_partial, 'chan').astype(jnp.bfloat16)  87.6 us
    dot_general x2, matrix products, contract_rows(): lax.dot_general(left, right, (((0,), (0,)), ((), ())), preferred_element_...  21.4 us
    dot_general x1, matrix products, local(): lax.dot_general(acts, proj_b, (((1,), (1,)), ((), ())), preferred_element...  13.4 us
  transfers between devices with their start and end apart: 2, of which 1 were waited for; matrix products, arithmetic and copies ran while one was open for 5% of the time, Pallas kernels for 0%

commit v1 on v0

v1 whole, which is shorter than its diff:
```python
import functools

import jax
import jax.numpy as jnp
from jax import lax
from jax.experimental import pallas as pl
from jax.experimental.pallas import tpu as pltpu
from jax.sharding import PartitionSpec as P

MESH = pl.DeviceIdType.MESH


def reduce_gather_kernel(
    chips, groups, x_ref, out_ref, pair, mine, slots, reduced, total,
    pair_send, pair_recv, rs_send, rs_recv, tok_send, tok_recv,
    ag_send, ag_recv, fwd_send, fwd_recv,
):
    me = lax.axis_index("chan")
    chip, core = me // 2, me % 2
    other = 1 - core
    partner = chip * 2 + other
    tok = lax.axis_index("tok")

    def peer(step):
        return lax.rem(chip + step, chips)

    def group(step):
        return lax.rem(tok + step, groups)

    barrier = pltpu.get_barrier_semaphore()
    pl.semaphore_signal(barrier, inc=1, device_id={"chan": partner}, device_id_type=MESH)
    for step in range(1, chips):
        pl.semaphore_signal(
            barrier, inc=1, device_id={"chan": peer(step) * 2 + core}, device_id_type=MESH
        )
    for step in range(1, groups):
        pl.semaphore_signal(barrier, inc=1, device_id={"tok": group(step)}, device_id_type=MESH)
    pl.semaphore_wait(barrier, chips + groups - 1)

    order = [(chips // 2 + step) % chips for step in range(chips)]
    order = [step for step in order if step] + [0]

    def pair_copy(step):
        slot = peer(step)
        return pltpu.make_async_remote_copy(
            x_ref.at[:, other, slot], pair.at[slot], pair_send.at[slot], pair_recv.at[slot],
            device_id={"chan": partner}, device_id_type=MESH,
        )

    for step in order:
        pair_copy(step).start()

    def rs_copy(step, landed):
        slot = peer(step)
        return pltpu.make_async_remote_copy(
            mine.at[slot], slots.at[landed], rs_send.at[slot], rs_recv.at[landed],
            device_id={"chan": slot * 2 + core}, device_id_type=MESH,
        )

    for step in order:
        slot = peer(step)
        pair_copy(step).wait_recv()
        value = x_ref[:, core, slot] + pair[slot]
        if step:
            mine[slot] = value.astype(jnp.bfloat16)
            rs_copy(step, chip).start()
        else:
            total[...] = value
    for step in range(1, chips):
        slot = peer(step)
        rs_copy(step, slot).wait_recv()
        total[...] += slots[slot].astype(jnp.float32)

    if groups == 1:
        out_ref[:, core, chip] = total[...].astype(jnp.bfloat16)
    else:
        reduced[...] = total[...].astype(jnp.bfloat16)

        def tok_copy(step, landed):
            target = group(step)
            return pltpu.make_async_remote_copy(
                reduced.at[target], out_ref.at[landed, core, chip],
                tok_send.at[target], tok_recv.at[landed],
                device_id={"tok": target}, device_id_type=MESH,
            )

        for step in range(1, groups):
            tok_copy(step, tok).start()
        out_ref[tok, core, chip] = reduced[tok]
        for step in range(1, groups):
            tok_copy(step, group(step)).wait_recv()

    def ag_copy(step, landed):
        block = out_ref.at[:, core, landed]
        slot = peer(step)
        return pltpu.make_async_remote_copy(
            block, block, ag_send.at[slot], ag_recv.at[landed],
            device_id={"chan": slot * 2 + core}, device_id_type=MESH,
        )

    def fwd_copy(slot, side):
        block = out_ref.at[:, side, slot]
        return pltpu.make_async_remote_copy(
            block, block, fwd_send.at[slot], fwd_recv.at[slot],
            device_id={"chan": partner}, device_id_type=MESH,
        )

    for step in order[:-1]:
        ag_copy(step, chip).start()
    fwd_copy(chip, core).start()
    for step in range(1, chips):
        slot = peer(step)
        ag_copy(step, slot).wait_recv()
        fwd_copy(slot, core).start()
    for step in range(chips):
        fwd_copy(peer(step), other).wait_recv()

    for step in range(chips):
        pair_copy(step).wait_send()
        fwd_copy(peer(step), core).wait_send()
        if step:
            rs_copy(step, chip).wait_send()
            ag_copy(step, chip).wait_send()
    if groups > 1:
        for step in range(1, groups):
            tok_copy(step, tok).wait_send()


def reduce_gather(x, devices, groups, collective_id):
    rows, tokens = x.shape
    chips = devices // 2
    part = rows // (devices * groups)
    shape = (groups, 2, chips, part, tokens)
    block = (groups, part, tokens)
    vmem = pl.BlockSpec(memory_space=pltpu.VMEM)
    dma = pltpu.SemaphoreType.DMA
    return pl.pallas_call(
        functools.partial(reduce_gather_kernel, chips, groups),
        out_shape=jax.ShapeDtypeStruct(shape, jnp.bfloat16),
        in_specs=[vmem],
        out_specs=vmem,
        scratch_shapes=[
            pltpu.VMEM((chips,) + block, jnp.float32),
            pltpu.VMEM((chips,) + block, jnp.bfloat16),
            pltpu.VMEM((chips,) + block, jnp.bfloat16),
            pltpu.VMEM(block, jnp.bfloat16),
            pltpu.VMEM(block, jnp.float32),
            dma((chips,)), dma((chips,)),
            dma((chips,)), dma((chips,)),
            dma((groups,)), dma((groups,)),
            dma((chips,)), dma((chips,)),
            dma((chips,)), dma((chips,)),
        ],
        compiler_params=pltpu.CompilerParams(
            collective_id=collective_id, has_side_effects=True, vmem_limit_bytes=32 * 2**20
        ),
        cost_estimate=pl.CostEstimate(
            flops=4 * rows * tokens, bytes_accessed=8 * rows * tokens, transcendentals=0
        ),
    )(x.reshape(shape))


def local(acts, target, proj_b, proj_a):
    toks, chans = lax.axis_size("tok"), lax.axis_size("chan")
    tok = lax.axis_index("tok")
    tokens, rank = acts.shape[0], proj_b.shape[0]
    factor_scale = -2.0 / (tokens * toks)
    acts_all = lax.all_gather(acts, "tok", axis=0, tiled=True)

    codes_part = lax.dot_general(
        proj_b, acts, (((1,), (1,)), ((), ())), preferred_element_type=jnp.float32
    )
    codes = reduce_gather(codes_part, chans, 1, 0).reshape(rank, tokens)
    predicted = lax.dot_general(
        codes, proj_a, (((0,), (1,)), ((), ())), preferred_element_type=jnp.float32
    )
    residual = (target.astype(jnp.float32) - predicted).astype(jnp.bfloat16)
    grad_part = lax.dot_general(
        proj_a, residual, (((0,), (1,)), ((), ())), preferred_element_type=jnp.float32
    )
    grad_codes = reduce_gather(grad_part, chans, toks, 1)

    share = rank // toks

    def term_a(step):
        rows = lax.dynamic_slice_in_dim(codes, (tok ^ step) * share, share, 0)
        return lax.dot_general(
            residual, rows, (((0,), (1,)), ((), ())), preferred_element_type=jnp.float32
        )

    grad_a = term_a(0)
    for step in range(1, toks):
        sent = lax.ppermute(
            term_a(step).astype(jnp.bfloat16), "tok", [(t, t ^ step) for t in range(toks)]
        )
        grad_a = grad_a + sent.astype(jnp.float32)

    grad_codes = grad_codes.reshape(toks, share, tokens).transpose(1, 0, 2)
    grad_b = jnp.dot(
        grad_codes.reshape(share, toks * tokens), acts_all, preferred_element_type=jnp.float32
    )
    return (grad_a * factor_scale, grad_b * factor_scale)


def solution(mesh):
    return jax.shard_map(
        local,
        mesh=mesh,
        in_specs=(P("tok", "chan"), P("tok", "chan"), P(None, "chan"), P("chan", None)),
        out_specs=(P("chan", "tok"), P("tok", "chan")),
        check_vma=False,
    )
```

time: 504 us -> 232 us (0.46)
  waiting for transfers between devices: 252 us -> 0.69 us
  blocking collectives: 178 us -> 0 us
  Pallas kernels: 0 us -> 156 us
  other arithmetic: 9.86 us -> 0 us
  local copies, waits for them, and re-layouts: 2.84 us -> 9.96 us
    reduce_scatter x2 -> x0, waiting for transfers between devices: 252 us -> none  [the longest x1 252 us: local(): lax.psum_scatter(contract_rows(grad_codes, acts), 'tok', scatter_dimensio...]
    psum x2 -> x0, blocking collectives: 178 us -> none  [the longest x1 90.8 us: local(): codes = lax.psum(partial_value, 'chan').astype(jnp.bfloat16)]
    pallas_call x0 -> x2, Pallas kernels: none -> 156 us  [reduce_gather(): pl.pallas_call(functools.partial(reduce_gather_kernel, chips, groups), ou...]
    mul x2 -> x0, other arithmetic: 9.86 us -> none  [the longest x1 6.72 us: local(): lax.psum_scatter(contract_rows(grad_codes, acts), 'tok', scatter_dimensio...]
    dot_general x0 -> x1, local copies, waits for them, and re-layouts: none -> 5.39 us  [local(): lax.dot_general(proj_a, residual, (((0,), (1,)), ((), ())), preferred_ele...]
    dot_general x5 -> x8, matrix products: 46 us -> 43.8 us  [the longest x1 13.2 us: local(): jnp.dot(grad_codes.reshape(share, toks * tokens), acts_all, preferred_ele...]
  transfers between devices with their start and end apart: 2 -> 4, of which waited for: 1 -> 0; matrix products, arithmetic and copies ran while one was open for 5% -> 17% of each run, Pallas kernels for 0% -> 68%
where the time goes in v1:
time: 232 us; the launch traced here: 228 us
  Pallas kernels  156 us (67%)
  matrix products  43.8 us (19%)
  between operations  14.1 us (6%)
  local copies, waits for them, and re-layouts  9.96 us (4%)
  starting transfers between devices  3.55 us (2%)
    pallas_call x2, Pallas kernels, reduce_gather(): pl.pallas_call(functools.partial(reduce_gather_kernel, chips, groups), ou...  156 us
    dot_general x1, matrix products, local(): jnp.dot(grad_codes.reshape(share, toks * tokens), acts_all, preferred_ele...  13.2 us
    dot_general x1, matrix products, local(): lax.dot_general(proj_b, acts, (((1,), (1,)), ((), ())), preferred_element...  11.9 us
    dot_general x4, matrix products, term_a(): lax.dot_general(residual, rows, (((0,), (1,)), ((), ())), preferred_eleme...  9.86 us
    dot_general x1, matrix products, local(): lax.dot_general(proj_a, residual, (((0,), (1,)), ((), ())), preferred_ele...  6.54 us
    dot_general x1, local copies, waits for them, and re-layouts, local(): lax.dot_general(proj_a, residual, (((0,), (1,)), ((), ())), preferred_ele...  5.39 us
  transfers between devices with their start and end apart: 4, of which 0 were waited for; matrix products, arithmetic and copies ran while one was open for 17% of the time, Pallas kernels for 68%

profile of v1, /device:TPU:0, one launch (start us, length us, event | category | flops | bytes accessed | tf_op | source)
XLA Modules:
  0.0 228.2 jit_solution(10869774412912202648)
XLA Ops:
  7.2 0.0 all-gather.2.cloned.1.call-start
  7.2 0.7 all-gather.2.cloned.1.call-update
  7.9 11.9 %fusion.11 = f32[2048,512]{1,0:T(8,128)S(1)} fusion(bf16[2048,3584]{1,0:T(8,128)(2,1)} %param.6, bf16[512,3584]{1,0:T(8,128)(2,1)} %param.4), kind=kOutput, calls=%fused_computation.16 | convolution fusion | flops 7516192768 | bytes 22544384 | tf_op jit(solution)/shard_map/dot_general | solution.py:170
  19.8 0.0 copy-start.3
  19.8 0.0 copy-start.4
  19.8 57.2 %shard_map.59 = bf16[1,2,4,256,512]{4,3,2,1,0:T(8,128)(2,1)S(1)} custom-call(f32[1,2,4,256,512]{4,3,2,1,0:T(8,128)S(1)} %bitcast.23), custom_call_target="tpu_custom_call" | custom-call | flops 4194304 | bytes 8388608 | tf_op jit(solution)/shard_map/pallas_call | solution.py:137
  77.0 0.0 copy-start.1
  77.1 0.0 copy-done.3
  77.1 0.0 copy-done.4
  77.1 2.4 %subtract_convert_fusion = bf16[512,1024]{1,0:T(8,128)(2,1)S(1)} fusion(bf16[512,1024]{1,0:T(8,128)(2,1)S(1)} %copy-done.4, bf16[2048,512]{1,0:T(8,128)(2,1)S(1)} %bitcast.24, bf16[1024,2048]{1,0:T(8,128)(2,1)S(1)} %copy-done.3), kind=kOutput, calls=%fused_computation.3 | convolution fusion | flops 2149056512 | bytes 8388608 | tf_op jit(solution)/shard_map/dot_general | solution.py:174
  79.5 1.8 convolution_convert_fusion.2
  81.3 1.5 collective-permute-start
  82.8 1.8 convolution_convert_fusion.1
  84.6 1.5 collective-permute-start.1
  86.1 0.0 copy-done.1
  86.1 1.7 convolution_convert_fusion
  87.8 0.5 collective-permute-start.2
  88.3 6.5 %convolution_bitcast_fusion = f32[2048,512]{0,1:T(8,128)} fusion(bf16[512,1024]{1,0:T(8,128)(2,1)S(1)} %subtract_convert_fusion, bf16[1024,2048]{1,0:T(8,128)(2,1)} %param.7), kind=kOutput, calls=%fused_computation.1 | convolution fusion | flops 2147483648 | bytes 9437184 | tf_op jit(solution)/shard_map/dot_general | solution.py:178
  94.9 5.4 %copy.7 = f32[2048,512]{1,0:T(8,128)} copy(f32[2048,512]{0,1:T(8,128)} %convolution_bitcast_fusion) | data formatting | bytes 8388608 | tf_op jit(solution)/shard_map/dot_general | solution.py:178
  100.2 0.0 copy-start
  100.2 2.2 copy-done
  102.4 98.8 %shard_map.60 = bf16[4,2,4,64,512]{4,3,2,1,0:T(8,128)(2,1)S(1)} custom-call(f32[4,2,4,64,512]{4,3,2,1,0:T(8,128)S(1)} %bitcast.21), custom_call_target="tpu_custom_call" | custom-call | flops 4194304 | bytes 8388608 | tf_op jit(solution)/shard_map/pallas_call | solution.py:137
  201.2 2.4 %copy.8 = bf16[4,512,512]{1,2,0:T(8,128)(2,1)} copy(bf16[4,512,512]{2,1,0:T(8,128)(2,1)S(1)} %bitcast.22) | data formatting | bytes 4194304 | tf_op jit(solution)/shard_map/reshape | solution.py:198
  203.6 0.0 copy-start.2
  203.6 0.0 collective-permute-done
  203.6 0.0 collective-permute-done.1
  203.6 0.0 collective-permute-done.2
  203.6 4.5 %add_multiply_fusion = f32[1024,512]{1,0:T(8,128)} fusion(bf16[1024,512]{1,0:T(8,128)(2,1)} %collective-permute-done.2, bf16[1024,512]{1,0:T(8,128)(2,1)} %collective-permute-done.1, bf16[1024,512]{1,0:T(8,128)(2,1)} %collective-permute-done, bf16[512,1024]{1,0:T(8,128)(2,1)S(1)} %subtract_convert_fusion, bf16[2048,512]{1,0:T(8,128)(2,1)} %bitcast.28, ...), kind=kOutput, calls=%fused_computation.2 | convolution fusion | flops 540540928 | bytes 6815748 | tf_op jit(solution)/shard_map/dot_general | solution.py:187
  208.1 0.0 all-gather.2.cloned.1.call-done
  208.1 0.0 copy-done.2
  208.1 13.2 %convolution_multiply_fusion = f32[512,3584]{1,0:T(8,128)} fusion(bf16[512,2048]{0,1:T(8,128)(2,1)S(1)} %bitcast.29, bf16[2048,3584]{1,0:T(8,128)(2,1)} %all-gather.2.cloned.1.call-done), kind=kOutput, calls=%fused_computation | convolution fusion | flops 7518027776 | bytes 24117248 | tf_op jit(solution)/shard_map/dot_general | solution.py:199
Async XLA Ops:
  7.2 201.0 %all-gather.2.cloned.1.call-start = ((), (), s32[]{:S(2)}) async-start(), calls=%async_computation | async-start | bytes 18350080 | tf_op jit(solution)/shard_map/all_gather | solution.py:168
  19.8 57.3 %copy-start.3 = (bf16[1024,2048]{1,0:T(8,128)(2,1)S(1)}, bf16[1024,2048]{1,0:T(8,128)(2,1)}, u32[]{:S(2)}) copy-start(bf16[1024,2048]{1,0:T(8,128)(2,1)} %param.7) | copy-start | bytes 12582916
  19.8 57.3 %copy-start.4 = (bf16[512,1024]{1,0:T(8,128)(2,1)S(1)}, bf16[512,1024]{1,0:T(8,128)(2,1)}, u32[]{:S(2)}) copy-start(bf16[512,1024]{1,0:T(8,128)(2,1)} %param.5) | copy-start | bytes 3145732
  77.0 9.1 %copy-start.1 = (bf16[1,2,4,256,512]{4,3,2,1,0:T(8,128)(2,1)}, bf16[1,2,4,256,512]{4,3,2,1,0:T(8,128)(2,1)S(1)}, u32[]{:S(2)}) copy-start(bf16[1,2,4,256,512]{4,3,2,1,0:T(8,128)(2,1)S(1)} %shard_map.59) | copy-start | bytes 6291460
  81.3 122.3 %collective-permute-start = (bf16[1024,512]{1,0:T(8,128)(2,1)}, bf16[1024,512]{1,0:T(8,128)(2,1)}, u32[]{:S(2)}, u32[]{:S(2)}) collective-permute-start(bf16[1024,512]{1,0:T(8,128)(2,1)} %convolution_convert_fusion.2), channel_id=1, source_target_pairs={{0,8},{8,0},{16,24},{24,16},{1,9},{9,1},{17,25},{25,17},{2,10},{10... | collective-permute-start | bytes 3145736 | tf_op jit(solution)/shard_map/ppermute | solution.py:193
  84.6 119.0 %collective-permute-start.1 = (bf16[1024,512]{1,0:T(8,128)(2,1)}, bf16[1024,512]{1,0:T(8,128)(2,1)}, u32[]{:S(2)}, u32[]{:S(2)}) collective-permute-start(bf16[1024,512]{1,0:T(8,128)(2,1)} %convolution_convert_fusion.1), channel_id=1, source_target_pairs={{0,16},{8,24},{16,0},{24,8},{1,17},{9,25},{17,1},{25,9},{2,18},{10... | collective-permute-start | bytes 3145736 | tf_op jit(solution)/shard_map/ppermute | solution.py:193
  87.8 115.8 %collective-permute-start.2 = (bf16[1024,512]{1,0:T(8,128)(2,1)}, bf16[1024,512]{1,0:T(8,128)(2,1)}, u32[]{:S(2)}, u32[]{:S(2)}) collective-permute-start(bf16[1024,512]{1,0:T(8,128)(2,1)} %convolution_convert_fusion), channel_id=1, source_target_pairs={{0,24},{8,16},{16,8},{24,0},{1,25},{9,17},{17,9},{25,1},{2,26},{10... | collective-permute-start | bytes 3145736 | tf_op jit(solution)/shard_map/ppermute | solution.py:193
  100.2 2.2 copy-start
  203.6 4.5 %copy-start.2 = (bf16[4,512,512]{1,2,0:T(8,128)(2,1)S(1)}, bf16[4,512,512]{1,2,0:T(8,128)(2,1)}, u32[]{:S(2)}) copy-start(bf16[4,512,512]{1,2,0:T(8,128)(2,1)} %copy.8) | copy-start | bytes 6291460
Sparse Core Ops, SparseCore 0:
  9.8 190.4 all-gather.1

commit v2 on v1

v2 whole, which is shorter than its diff:
```python
import functools

import jax
import jax.numpy as jnp
from jax import lax
from jax.experimental import pallas as pl
from jax.experimental.pallas import tpu as pltpu
from jax.sharding import PartitionSpec as P

MESH = pl.DeviceIdType.MESH


def reduce_gather_kernel(
    chips, groups, *refs
):
    if groups == 1:
        x_ref, out_ref = refs[:2]
        refs = refs[2:]
    else:
        codes_ref, a_ref, target_ref, out_ref, grad_ref = refs[:5]
        x_ref, res_ref, term_out, term_in, term_send, term_recv = refs[-6:]
        refs = refs[5:-6]
    (
        pair, mine, slots, reduced, total, pair_send, pair_recv, rs_send, rs_recv,
        tok_send, tok_recv, ag_send, ag_recv, fwd_send, fwd_recv,
    ) = refs
    me = lax.axis_index("chan")
    chip, core = me // 2, me % 2
    other = 1 - core
    partner = chip * 2 + other
    tok = lax.axis_index("tok")

    def peer(step):
        return lax.rem(chip + step, chips)

    def group(step):
        return tok ^ step

    barrier = pltpu.get_barrier_semaphore()
    pl.semaphore_signal(barrier, inc=1, device_id={"chan": partner}, device_id_type=MESH)
    for step in range(1, chips):
        pl.semaphore_signal(
            barrier, inc=1, device_id={"chan": peer(step) * 2 + core}, device_id_type=MESH
        )
    for step in range(1, groups):
        pl.semaphore_signal(barrier, inc=1, device_id={"tok": group(step)}, device_id_type=MESH)
    pl.semaphore_wait(barrier, chips + groups - 1)

    size = 256
    if groups > 1:
        @pl.loop(0, a_ref.shape[0] // size)
        def _(index):
            block = pl.ds(pl.multiple_of(index * size, size), size)
            predicted = jnp.dot(
                a_ref[block], codes_ref[...], preferred_element_type=jnp.float32
            )
            wanted = target_ref[:, block].astype(jnp.float32).T
            res_ref[block] = (wanted - predicted).astype(jnp.bfloat16)

    def make_x(side):
        rows = x_ref.shape[2] * x_ref.shape[3]

        @pl.loop(0, groups)
        def _(index):
            columns = pl.ds(pl.multiple_of((index * 2 + side) * rows, rows), rows)
            part = lax.dot_general(
                a_ref[:, columns], res_ref[...], (((0,), (0,)), ((), ())),
                preferred_element_type=jnp.float32,
            )
            x_ref[index, side] = part.reshape(x_ref.shape[2:])

    if groups > 1:
        make_x(other)

    order = [(chips // 2 + step) % chips for step in range(chips)]
    order = [step for step in order if step] + [0]

    def pair_copy(step):
        slot = peer(step)
        return pltpu.make_async_remote_copy(
            x_ref.at[:, other, slot], pair.at[slot], pair_send.at[slot], pair_recv.at[slot],
            device_id={"chan": partner}, device_id_type=MESH,
        )

    for step in order:
        pair_copy(step).start()

    if groups > 1:
        make_x(core)

    def rs_copy(step, landed):
        slot = peer(step)
        return pltpu.make_async_remote_copy(
            mine.at[slot], slots.at[landed], rs_send.at[slot], rs_recv.at[landed],
            device_id={"chan": slot * 2 + core}, device_id_type=MESH,
        )

    for step in order:
        slot = peer(step)
        pair_copy(step).wait_recv()
        value = x_ref[:, core, slot] + pair[slot]
        if step:
            mine[slot] = value.astype(jnp.bfloat16)
            rs_copy(step, chip).start()
        else:
            total[...] = value

    def term(step, block):
        share = grad_ref.shape[1]
        rows = codes_ref[pl.ds(pl.multiple_of(group(step) * share, share), share)]
        return lax.dot_general(
            res_ref[block], rows, (((1,), (1,)), ((), ())), preferred_element_type=jnp.float32
        )

    if groups > 1:

        @pl.loop(0, res_ref.shape[0] // size)
        def _(index):
            block = pl.ds(pl.multiple_of(index * size, size), size)
            for step in range(1, groups):
                term_out[step - 1, block] = term(step, block).astype(jnp.bfloat16)
            grad_ref[block] = term(0, block)

    for step in range(1, chips):
        slot = peer(step)
        rs_copy(step, slot).wait_recv()
        total[...] += slots[slot].astype(jnp.float32)

    if groups == 1:
        out_ref[:, core, chip] = total[...].astype(jnp.bfloat16)
    else:
        reduced[...] = total[...].astype(jnp.bfloat16)

        def tok_copy(step):
            target = group(step)
            return pltpu.make_async_remote_copy(
                reduced.at[target], out_ref.at[step, core, chip],
                tok_send.at[step], tok_recv.at[step],
                device_id={"tok": target}, device_id_type=MESH,
            )

        def term_copy(step):
            return pltpu.make_async_remote_copy(
                term_out.at[step - 1], term_in.at[step - 1],
                term_send.at[step - 1], term_recv.at[step - 1],
                device_id={"tok": group(step)}, device_id_type=MESH,
            )

        for step in range(1, groups):
            tok_copy(step).start()
        out_ref[0, core, chip] = reduced[tok]
        for step in range(1, groups):
            tok_copy(step).wait_recv()

    def ag_copy(step, landed):
        block = out_ref.at[:, core, landed]
        slot = peer(step)
        return pltpu.make_async_remote_copy(
            block, block, ag_send.at[slot], ag_recv.at[landed],
            device_id={"chan": slot * 2 + core}, device_id_type=MESH,
        )

    def fwd_copy(slot, side):
        block = out_ref.at[:, side, slot]
        return pltpu.make_async_remote_copy(
            block, block, fwd_send.at[slot], fwd_recv.at[slot],
            device_id={"chan": partner}, device_id_type=MESH,
        )

    for step in order[:-1]:
        ag_copy(step, chip).start()
    fwd_copy(chip, core).start()
    if groups > 1:
        for step in reversed(range(1, groups)):
            term_copy(step).start()
    for step in range(1, chips):
        slot = peer(step)
        ag_copy(step, slot).wait_recv()
        fwd_copy(slot, core).start()
    for step in range(chips):
        fwd_copy(peer(step), other).wait_recv()

    for step in range(chips):
        pair_copy(step).wait_send()
        fwd_copy(peer(step), core).wait_send()
        if step:
            rs_copy(step, chip).wait_send()
            ag_copy(step, chip).wait_send()
    if groups > 1:
        for step in range(1, groups):
            tok_copy(step).wait_send()
            term_copy(step).wait_send()
            term_copy(step).wait_recv()
            grad_ref[...] += term_in[step - 1].astype(jnp.float32)


def reduce_gather(operands, devices, groups, collective_id):
    rows, tokens = operands[0].shape
    chips = devices // 2
    part = rows // (devices * groups)
    shape = (groups, 2, chips, part, tokens)
    block = (groups, part, tokens)
    vmem = pl.BlockSpec(memory_space=pltpu.VMEM)
    dma = pltpu.SemaphoreType.DMA
    out_shape = [jax.ShapeDtypeStruct(shape, jnp.bfloat16)]
    extra, flops = [], 4 * rows * tokens
    if groups > 1:
        channels = operands[1].shape[0]
        term = (channels, rows // groups)
        out_shape.append(jax.ShapeDtypeStruct(term, jnp.float32))
        extra = [
            pltpu.VMEM(shape, jnp.float32),
            pltpu.VMEM((channels, tokens), jnp.bfloat16),
            pltpu.VMEM((groups - 1,) + term, jnp.bfloat16),
            pltpu.VMEM((groups - 1,) + term, jnp.bfloat16),
            dma((groups - 1,)), dma((groups - 1,)),
        ]
        flops = 6 * rows * tokens * channels
    else:
        operands = [operands[0].reshape(shape)]
    return pl.pallas_call(
        functools.partial(reduce_gather_kernel, chips, groups),
        out_shape=out_shape,
        in_specs=[vmem] * len(operands),
        out_specs=[vmem] * len(out_shape),
        scratch_shapes=[
            pltpu.VMEM((chips,) + block, jnp.float32),
            pltpu.VMEM((chips,) + block, jnp.bfloat16),
            pltpu.VMEM((chips,) + block, jnp.bfloat16),
            pltpu.VMEM(block, jnp.bfloat16),
            pltpu.VMEM(block, jnp.float32),
            dma((chips,)), dma((chips,)),
            dma((chips,)), dma((chips,)),
            dma((groups,)), dma((groups,)),
            dma((chips,)), dma((chips,)),
            dma((chips,)), dma((chips,)),
        ] + extra,
        compiler_params=pltpu.CompilerParams(
            collective_id=collective_id, has_side_effects=True, vmem_limit_bytes=48 * 2**20
        ),
        cost_estimate=pl.CostEstimate(
            flops=flops, bytes_accessed=8 * rows * tokens, transcendentals=0
        ),
    )(*operands)


def grad_b_kernel(places, scale, codes_ref, *refs):
    out_ref, total = refs[-1], None
    for (step, start), piece in zip(places, refs):
        term = jnp.dot(
            codes_ref[step, :, start : start + piece.shape[0]], piece[...],
            preferred_element_type=jnp.float32,
        )
        total = term if total is None else total + term
    out_ref[...] = total * scale


def grad_b_of(grad_codes, pieces, places, scale):
    share, columns = grad_codes.shape[1], pieces[0].shape[1]
    width = 512 if columns % 512 == 0 else 256
    tokens = sum(piece.shape[0] for piece in pieces)
    return pl.pallas_call(
        functools.partial(grad_b_kernel, places, scale),
        grid=(columns // width,),
        out_shape=jax.ShapeDtypeStruct((share, columns), jnp.float32),
        in_specs=[pl.BlockSpec(grad_codes.shape, lambda i: (0, 0, 0))]
        + [pl.BlockSpec((piece.shape[0], width), lambda i: (0, i)) for piece in pieces],
        out_specs=pl.BlockSpec((share, width), lambda i: (0, i)),
        compiler_params=pltpu.CompilerParams(vmem_limit_bytes=48 * 2**20),
        cost_estimate=pl.CostEstimate(
            flops=2 * share * columns * tokens,
            bytes_accessed=columns * (2 * tokens + 4 * share),
            transcendentals=0,
        ),
    )(grad_codes, *pieces)


def gather_start(acts, toks):
    if toks != 4:
        return [lax.all_gather(acts, "tok", axis=0, tiled=False)]
    return [
        lax.ppermute(acts, "tok", [(t, t ^ step) for t in range(toks)]) for step in (1, 2)
    ]


def gather_end(acts, begun, toks, tok):
    tokens = acts.shape[0]
    if toks != 4:
        (whole,) = begun
        pieces = [acts] + [
            lax.dynamic_index_in_dim(whole, tok ^ step, 0, keepdims=False)
            for step in range(1, toks)
        ]
        return [(step, 0) for step in range(toks)], pieces

    def move(x, step):
        return lax.ppermute(x, "tok", [(t, t ^ step) for t in range(toks)])

    half = tokens // 2
    along_x, along_y = begun
    low, high = move(along_x[:half], 2), move(along_y[half:], 1)
    return [(0, 0), (1, 0), (2, 0), (3, 0), (3, half)], [acts, along_x, along_y, low, high]


def local(acts, target, proj_b, proj_a):
    toks, chans = lax.axis_size("tok"), lax.axis_size("chan")
    tok = lax.axis_index("tok")
    tokens, rank = acts.shape[0], proj_b.shape[0]
    factor_scale = -2.0 / (tokens * toks)
    begun = gather_start(acts, toks)

    codes_part = lax.dot_general(
        proj_b, acts, (((1,), (1,)), ((), ())), preferred_element_type=jnp.float32
    )
    codes = reduce_gather([codes_part], chans, 1, 0)[0].reshape(rank, tokens)
    codes, begun = lax.optimization_barrier((codes, begun))
    places, pieces = gather_end(acts, begun, toks, tok)
    grad_codes, grad_a = reduce_gather([codes, proj_a, target], chans, toks, 1)
    grad_codes = grad_codes.reshape(toks, rank // toks, tokens)
    grad_b = grad_b_of(grad_codes, pieces, places, factor_scale)
    return (grad_a * factor_scale, grad_b)


def solution(mesh):
    return jax.shard_map(
        local,
        mesh=mesh,
        in_specs=(P("tok", "chan"), P("tok", "chan"), P(None, "chan"), P("chan", None)),
        out_specs=(P("chan", "tok"), P("tok", "chan")),
        check_vma=False,
    )
```

time: 232 us -> 193 us (0.83); the launches traced: 228 us -> 192 us
  matrix products: 43.8 us -> 13.4 us
  between operations: 14.1 us -> 0.68 us
  waiting for transfers between devices: 0.69 us -> 9.07 us
  local copies, waits for them, and re-layouts: 9.96 us -> 1.95 us
  starting transfers between devices: 3.55 us -> 7.25 us
    dot_general x7 -> x0, matrix products: 32 us -> none  [the longest x1 13.2 us: local(): jnp.dot(grad_codes.reshape(share, toks * tokens), acts_all, preferred_ele...]
    pallas_call x0 -> x1, Pallas kernels: none -> 12.7 us  [grad_b_of(): pl.pallas_call(functools.partial(grad_b_kernel, places, scale), grid=(col...]
    pallas_call x2, Pallas kernels: 156 us -> 146 us  [reduce_gather(): pl.pallas_call(functools.partial(reduce_gather_kernel, chips, groups), ou...]
    ppermute x3 -> x4, waiting for transfers between devices: 0.01 us -> 9.07 us  [the longest x2 9.07 us: gather_start(): lax.ppermute(acts, 'tok', [(t, t ^ step) for t in range(toks)])]
    dot_general x1 -> x0, local copies, waits for them, and re-layouts: 5.39 us -> none  [local(): lax.dot_general(proj_a, residual, (((0,), (1,)), ((), ())), preferred_ele...]
    ppermute x3 -> x4, starting transfers between devices: 3.52 us -> 7.25 us  [the longest x2 4.52 us: gather_start(): lax.ppermute(acts, 'tok', [(t, t ^ step) for t in range(toks)])]
    reshape x1 -> x0, local copies, waits for them, and re-layouts: 2.36 us -> none  [local(): grad_codes = grad_codes.reshape(toks, share, tokens).transpose(1, 0, 2)]
  transfers between devices with their start and end apart: 4 -> 4, of which waited for: 0 -> 2; matrix products, arithmetic and copies ran while one was open for 17% -> 8% of each run, Pallas kernels for 68% -> 76%
where the time goes in v2:
time: 193 us; the launch traced here: 192 us
  Pallas kernels  158 us (82%)
  matrix products  13.4 us (7%)
  waiting for transfers between devices  9.07 us (5%)
  starting transfers between devices  7.25 us (4%)
  local copies, waits for them, and re-layouts  1.95 us (1%)
    pallas_call x2, Pallas kernels, reduce_gather(): pl.pallas_call(functools.partial(reduce_gather_kernel, chips, groups), ou...  146 us
    dot_general x1, matrix products, local(): lax.dot_general(proj_b, acts, (((1,), (1,)), ((), ())), preferred_element...  13.4 us
    pallas_call x1, Pallas kernels, grad_b_of(): pl.pallas_call(functools.partial(grad_b_kernel, places, scale), grid=(col...  12.7 us
    ppermute x2, waiting for transfers between devices, gather_start(): lax.ppermute(acts, 'tok', [(t, t ^ step) for t in range(toks)])  9.07 us
    ppermute x2, starting transfers between devices, gather_start(): lax.ppermute(acts, 'tok', [(t, t ^ step) for t in range(toks)])  4.52 us
  transfers between devices with their start and end apart: 4, of which 2 were waited for; matrix products, arithmetic and copies ran while one was open for 8% of the time, Pallas kernels for 76%

profile of v2, /device:TPU:0, one launch (start us, length us, event | category | flops | bytes accessed | tf_op | source)
XLA Modules:
  0.0 192.2 jit_solution(15652267598497905879)
XLA Ops:
  0.6 3.0 %collective-permute-start = (bf16[512,3584]{1,0:T(8,128)(2,1)}, bf16[512,3584]{1,0:T(8,128)(2,1)S(1)}, u32[]{:S(2)}, u32[]{:S(2)}) collective-permute-start(bf16[512,3584]{1,0:T(8,128)(2,1)} %refs_0_.1), channel_id=1, source_target_pairs={{0,8},{8,0},{16,24},{24,16},{1,9},{9,1},{17,25},{25,17},{2,10},{10... | collective-permute-start | bytes 11010056 | tf_op jit(solution)/shard_map/ppermute | solution.py:282
  3.6 1.5 collective-permute-start.1
  5.2 13.4 %fusion = f32[2048,512]{1,0:T(8,128)} fusion(bf16[2048,3584]{1,0:T(8,128)(2,1)} %param.6, bf16[512,3584]{1,0:T(8,128)(2,1)} %refs_0_.1), kind=kOutput, calls=%fused_computation.1 | convolution fusion | flops 7516192768 | bytes 22544384 | tf_op jit(solution)/shard_map/dot_general | solution.py:312
  18.6 57.0 %shard_map.59 = bf16[1,2,4,256,512]{4,3,2,1,0:T(8,128)(2,1)S(1)} custom-call(f32[1,2,4,256,512]{4,3,2,1,0:T(8,128)} %bitcast.7), custom_call_target="tpu_custom_call" | custom-call | flops 4194304 | bytes 8388608 | tf_op jit(solution)/shard_map/pallas_call | solution.py:221
  75.6 0.0 copy-start
  75.6 7.6 %collective-permute-done.refs_1_ = bf16[512,3584]{1,0:T(8,128)(2,1)S(1)} collective-permute-done((bf16[512,3584]{1,0:T(8,128)(2,1)}, bf16[512,3584]{1,0:T(8,128)(2,1)S(1)}, u32[]{:S(2)}, u32[]{:S(2)}) %collective-permute-start) | collective-permute-done | bytes 3670048 | tf_op jit(solution)/shard_map/ppermute | solution.py:282
  83.2 0.0 copy-start.2
  83.2 1.5 collective-permute-done.1.refs_2_
  84.6 0.0 copy-start.3
  84.6 0.0 copy-start.1
  84.6 0.1 slice.6
  84.8 1.7 copy-done.3
  86.5 0.1 slice.7
  86.6 0.0 copy-done
  86.6 0.0 copy-done.2
  86.6 1.2 collective-permute-start.3
  87.8 1.5 collective-permute-start.2
  89.3 0.0 copy-done.1
  89.3 88.6 %shard_map.60 = (bf16[4,2,4,64,512]{4,3,2,1,0:T(8,128)(2,1)S(1)}, f32[1024,512]{1,0:T(8,128)S(1)}) custom-call(bf16[2048,512]{1,0:T(8,128)(2,1)} %bitcast.5, bf16[1024,2048]{1,0:T(8,128)(2,1)} %refs_1_.1, bf16[512,1024]{1,0:T(8,128)(2,1)S(1)} %copy-done.1), custom_call_target="tpu_custom_call" | custom-call | flops 6442450944 | bytes 8388608 | tf_op jit(solution)/shard_map/pallas_call | solution.py:221
  178.0 1.6 broadcast_multiply_fusion
  179.5 0.0 collective-permute-done.3.refs_4_
  179.5 0.0 collective-permute-done.2.refs_3_
  179.5 12.7 %shard_map.61 = f32[512,3584]{1,0:T(8,128)} custom-call(bf16[4,512,512]{2,1,0:T(8,128)(2,1)S(1)} %bitcast.6, bf16[512,3584]{1,0:T(8,128)(2,1)} %refs_0_.1, bf16[512,3584]{1,0:T(8,128)(2,1)} %copy-done.2, bf16[512,3584]{1,0:T(8,128)(2,1)} %copy-done.3, bf16[256,3584]{1,0:T(8,128)(2,1)S(1)} %collective-permute-done.2.refs_3_, ...), custom_call_target="tpu_custom_call" | custom-call | flops 7516192768 | bytes 22020096 | tf_op jit(solution)/shard_map/pallas_call | solution.py:262
Async XLA Ops:
  0.6 82.6 %collective-permute-start = (bf16[512,3584]{1,0:T(8,128)(2,1)}, bf16[512,3584]{1,0:T(8,128)(2,1)S(1)}, u32[]{:S(2)}, u32[]{:S(2)}) collective-permute-start(bf16[512,3584]{1,0:T(8,128)(2,1)} %refs_0_.1), channel_id=1, source_target_pairs={{0,8},{8,0},{16,24},{24,16},{1,9},{9,1},{17,25},{25,17},{2,10},{10... | collective-permute-start | bytes 11010056 | tf_op jit(solution)/shard_map/ppermute | solution.py:282
  3.6 81.0 %collective-permute-start.1 = (bf16[512,3584]{1,0:T(8,128)(2,1)}, bf16[512,3584]{1,0:T(8,128)(2,1)S(1)}, u32[]{:S(2)}, u32[]{:S(2)}) collective-permute-start(bf16[512,3584]{1,0:T(8,128)(2,1)} %refs_0_.1), channel_id=1, source_target_pairs={{0,16},{8,24},{16,0},{24,8},{1,17},{9,25},{17,1},{25,9},{2,18},{10... | collective-permute-start | bytes 11010056 | tf_op jit(solution)/shard_map/ppermute | solution.py:282
  75.6 11.0 %copy-start = (bf16[1,2,4,256,512]{4,3,2,1,0:T(8,128)(2,1)}, bf16[1,2,4,256,512]{4,3,2,1,0:T(8,128)(2,1)S(1)}, u32[]{:S(2)}) copy-start(bf16[1,2,4,256,512]{4,3,2,1,0:T(8,128)(2,1)S(1)} %shard_map.59) | copy-start | bytes 6291460
  83.2 3.4 %copy-start.2 = (bf16[512,3584]{1,0:T(8,128)(2,1)}, bf16[512,3584]{1,0:T(8,128)(2,1)S(1)}, u32[]{:S(2)}) copy-start(bf16[512,3584]{1,0:T(8,128)(2,1)S(1)} %collective-permute-done.refs_1_) | copy-start | bytes 11010052
  84.6 1.8 copy-start.3
  84.6 4.7 %copy-start.1 = (bf16[512,1024]{1,0:T(8,128)(2,1)S(1)}, bf16[512,1024]{1,0:T(8,128)(2,1)}, u32[]{:S(2)}) copy-start(bf16[512,1024]{1,0:T(8,128)(2,1)} %refs_2_.1) | copy-start | bytes 3145732
  86.6 92.9 %collective-permute-start.3 = (bf16[256,3584]{1,0:T(8,128)(2,1)S(1)}, bf16[256,3584]{1,0:T(8,128)(2,1)S(1)}, u32[]{:S(2)}, u32[]{:S(2)}) collective-permute-start(bf16[256,3584]{1,0:T(8,128)(2,1)S(1)} %slice.7), channel_id=1, source_target_pairs={{0,8},{8,0},{16,24},{24,16},{1,9},{9,1},{17,25},{25,17},{2,10},{10... | collective-permute-start | bytes 5505032 | tf_op jit(solution)/shard_map/ppermute | solution.py:297
  87.8 91.7 %collective-permute-start.2 = (bf16[256,3584]{1,0:T(8,128)(2,1)S(1)}, bf16[256,3584]{1,0:T(8,128)(2,1)S(1)}, u32[]{:S(2)}, u32[]{:S(2)}) collective-permute-start(bf16[256,3584]{1,0:T(8,128)(2,1)S(1)} %slice.6), channel_id=1, source_target_pairs={{0,16},{8,24},{16,0},{24,8},{1,17},{9,25},{17,1},{25,9},{2,18},{10... | collective-permute-start | bytes 5505032 | tf_op jit(solution)/shard_map/ppermute | solution.py:297

commit v3 on v0

v3 whole, which is shorter than its diff:
```python
import functools

import jax
import jax.numpy as jnp
from jax import lax
from jax.experimental import pallas as pl
from jax.experimental.pallas import tpu as pltpu
from jax.sharding import PartitionSpec as P

MESH = pl.DeviceIdType.MESH


def partners():
    me = lax.axis_index("chan")
    chip, core = me // 2, me % 2
    return chip, core, chip * 2 + 1 - core


def greet(chips, groups):
    chip, core, partner = partners()
    barrier = pltpu.get_barrier_semaphore()
    pl.semaphore_signal(barrier, inc=1, device_id={"chan": partner}, device_id_type=MESH)
    for step in range(1, chips):
        there = lax.rem(chip + step, chips) * 2 + core
        pl.semaphore_signal(barrier, inc=1, device_id={"chan": there}, device_id_type=MESH)
    for step in range(1, groups):
        there = lax.axis_index("tok") ^ step
        pl.semaphore_signal(barrier, inc=1, device_id={"tok": there}, device_id_type=MESH)
    pl.semaphore_wait(barrier, chips + groups - 1)


def reduce_phase(chips, x_ref, make_x, beside, refs):
    pair, mine, slots, total, pair_send, pair_recv, rs_send, rs_recv = refs
    chip, core, partner = partners()
    other = 1 - core

    def peer(step):
        return lax.rem(chip + step, chips)

    order = [(chips // 2 + step) % chips for step in range(chips)]
    order = [step for step in order if step] + [0]

    def pair_copy(step):
        slot = peer(step)
        return pltpu.make_async_remote_copy(
            x_ref.at[:, other, slot], pair.at[slot], pair_send.at[slot], pair_recv.at[slot],
            device_id={"chan": partner}, device_id_type=MESH,
        )

    def rs_copy(step, landed):
        slot = peer(step)
        return pltpu.make_async_remote_copy(
            mine.at[slot], slots.at[landed], rs_send.at[slot], rs_recv.at[landed],
            device_id={"chan": slot * 2 + core}, device_id_type=MESH,
        )

    make_x(other)
    for step in order:
        pair_copy(step).start()
    make_x(core)
    for step in order:
        slot = peer(step)
        pair_copy(step).wait_recv()
        value = x_ref[:, core, slot] + pair[slot]
        if step:
            mine[slot] = value.astype(jnp.bfloat16)
            rs_copy(step, chip).start()
        else:
            total[...] = value
    beside()
    for step in range(1, chips):
        slot = peer(step)
        rs_copy(step, slot).wait_recv()
        total[...] += slots[slot].astype(jnp.float32)
    for step in range(chips):
        pair_copy(step).wait_send()
        if step:
            rs_copy(step, chip).wait_send()


def gather_phase(chips, out_ref, refs):
    right_send, left_send, ag_recv, fwd_send, fwd_recv = refs
    chip, core, partner = partners()

    def hop(slot, right):
        block = out_ref.at[:, core, slot]
        there = lax.rem(chip + (1 if right else chips - 1), chips)
        return pltpu.make_async_remote_copy(
            block, block, (right_send if right else left_send).at[slot], ag_recv.at[slot],
            device_id={"chan": there * 2 + core}, device_id_type=MESH,
        )

    def fwd_copy(slot, side):
        block = out_ref.at[:, side, slot]
        return pltpu.make_async_remote_copy(
            block, block, fwd_send.at[slot], fwd_recv.at[slot],
            device_id={"chan": partner}, device_id_type=MESH,
        )

    has_right, has_left = chip + 1 < chips, chip > 0

    @pl.when(has_right)
    def _():
        hop(chip, True).start()

    @pl.when(has_left)
    def _():
        hop(chip, False).start()

    fwd_copy(chip, core).start()
    for step in range(1, chips):

        @pl.when(chip >= step)
        def _():
            hop(chip - step, True).wait_recv()

            @pl.when(has_right)
            def _():
                hop(chip - step, True).start()

            fwd_copy(chip - step, core).start()

        @pl.when(chip + step < chips)
        def _():
            hop(chip + step, False).wait_recv()

            @pl.when(has_left)
            def _():
                hop(chip + step, False).start()

            fwd_copy(chip + step, core).start()

    for slot in range(chips):
        fwd_copy(slot, 1 - core).wait_recv()
        fwd_copy(slot, core).wait_send()

        @pl.when(has_right & (slot <= chip))
        def _():
            hop(slot, True).wait_send()

        @pl.when(has_left & (slot >= chip))
        def _():
            hop(slot, False).wait_send()


def codes_kernel(chips, x_ref, out_ref, *refs):
    greet(chips, 1)
    reduce_phase(chips, x_ref, lambda side: None, lambda: None, refs[:8])
    chip, core, _ = partners()
    out_ref[:, core, chip] = refs[3][...].astype(jnp.bfloat16)
    gather_phase(chips, out_ref, refs[8:])


def gather_kernel(chips, piece_ref, out_ref, *refs):
    greet(chips, 1)
    chip, core, _ = partners()
    out_ref[:, core, chip] = piece_ref[...]
    gather_phase(chips, out_ref, refs)


def term_place(groups, step, half):
    if groups != 4:
        return step - 1, half
    return {(1, 0): (0, 0), (3, 0): (0, 1), (2, 1): (1, 0), (3, 1): (1, 1),
            (2, 0): (2, 0), (1, 1): (2, 1)}[step, half]


def grads_kernel(chips, groups, codes_ref, a_ref, target_ref, piece_ref, own_ref, *refs):
    terms, refs = refs[: groups - 1], refs[groups - 1 :]
    x_ref, res_ref, reduced, tok_send, tok_recv = refs[8:]
    total = refs[3]
    tok = lax.axis_index("tok")
    greet(chips, groups)
    size = 256

    @pl.loop(0, a_ref.shape[0] // size)
    def _(index):
        block = pl.ds(pl.multiple_of(index * size, size), size)
        predicted = jnp.dot(a_ref[block], codes_ref[...], preferred_element_type=jnp.float32)
        wanted = target_ref[:, block].astype(jnp.float32).T
        res_ref[block] = (wanted - predicted).astype(jnp.bfloat16)

    def make_x(side):
        rows = x_ref.shape[2] * x_ref.shape[3]

        @pl.loop(0, groups)
        def _(index):
            columns = pl.ds(pl.multiple_of((index * 2 + side) * rows, rows), rows)
            part = lax.dot_general(
                a_ref[:, columns], res_ref[...], (((0,), (0,)), ((), ())),
                preferred_element_type=jnp.float32,
            )
            x_ref[index, side] = part.reshape(x_ref.shape[2:])

    def term(step, block):
        share = own_ref.shape[1]
        rows = codes_ref[pl.ds(pl.multiple_of((tok ^ step) * share, share), share)]
        return lax.dot_general(
            res_ref[block], rows, (((1,), (1,)), ((), ())), preferred_element_type=jnp.float32
        )

    def make_terms():
        length = terms[0].shape[1]
        chunk = min(size, length)
        for half in range(2):

            @pl.loop(0, length // chunk)
            def _(index):
                start = pl.multiple_of(index * chunk, chunk)
                block = pl.ds(pl.multiple_of(half * length + start, chunk), chunk)
                for step in range(1, groups):
                    array, place = term_place(groups, step, half)
                    value = term(step, block).astype(jnp.bfloat16)
                    terms[array][place, pl.ds(start, chunk)] = value
                own_ref[block] = term(0, block)

    reduce_phase(chips, x_ref, make_x, make_terms, refs[:8])
    reduced[...] = total[...].astype(jnp.bfloat16)

    def tok_copy(step):
        return pltpu.make_async_remote_copy(
            reduced.at[tok ^ step], piece_ref.at[step], tok_send.at[step], tok_recv.at[step],
            device_id={"tok": tok ^ step}, device_id_type=MESH,
        )

    for step in range(1, groups):
        tok_copy(step).start()
    piece_ref[0] = reduced[tok]
    for step in range(1, groups):
        tok_copy(step).wait_recv()
        tok_copy(step).wait_send()


def call(kernel, collective_id, operands, out_shape, scratch):
    vmem = pl.BlockSpec(memory_space=pltpu.VMEM)
    return pl.pallas_call(
        kernel,
        out_shape=out_shape,
        in_specs=[vmem] * len(operands),
        out_specs=[vmem] * len(out_shape),
        scratch_shapes=scratch,
        compiler_params=pltpu.CompilerParams(
            collective_id=collective_id, has_side_effects=True, vmem_limit_bytes=48 * 2**20
        ),
        cost_estimate=pl.CostEstimate(flops=0, bytes_accessed=1024, transcendentals=0),
    )(*operands)


def reduce_scratch(chips, block):
    dma = pltpu.SemaphoreType.DMA((chips,))
    return [
        pltpu.VMEM((chips,) + block, jnp.float32),
        pltpu.VMEM((chips,) + block, jnp.bfloat16),
        pltpu.VMEM((chips,) + block, jnp.bfloat16),
        pltpu.VMEM(block, jnp.float32),
    ] + [dma] * 4


def sum_codes(x, devices):
    rows, tokens = x.shape
    chips = devices // 2
    shape = (1, 2, chips, rows // devices, tokens)
    out = call(
        functools.partial(codes_kernel, chips), 0, [x.reshape(shape)],
        [jax.ShapeDtypeStruct(shape, jnp.bfloat16)],
        reduce_scratch(chips, (1,) + shape[3:]) + [pltpu.SemaphoreType.DMA((chips,))] * 5,
    )
    return out[0].reshape(rows, tokens)


def gather_codes(piece, devices):
    groups, part, tokens = piece.shape
    chips = devices // 2
    shape = (groups, 2, chips, part, tokens)
    out = call(
        functools.partial(gather_kernel, chips), 2, [piece],
        [jax.ShapeDtypeStruct(shape, jnp.bfloat16)],
        [pltpu.SemaphoreType.DMA((chips,))] * 5,
    )
    return out[0].reshape(groups, devices * part, tokens)


def grads(codes, proj_a, target, devices, groups):
    rows, tokens = codes.shape
    channels, chips = proj_a.shape[0], devices // 2
    block = (groups, rows // (devices * groups), tokens)
    share = rows // groups
    dma = pltpu.SemaphoreType.DMA((groups,))
    out = call(
        functools.partial(grads_kernel, chips, groups), 1, [codes, proj_a, target],
        [
            jax.ShapeDtypeStruct(block, jnp.bfloat16),
            jax.ShapeDtypeStruct((channels, share), jnp.float32),
        ]
        + [jax.ShapeDtypeStruct((2, channels // 2, share), jnp.bfloat16)] * (groups - 1),
        reduce_scratch(chips, block)
        + [
            pltpu.VMEM((groups, 2, chips) + block[1:], jnp.float32),
            pltpu.VMEM((channels, tokens), jnp.bfloat16),
            pltpu.VMEM(block, jnp.bfloat16),
            dma, dma,
        ],
    )
    return out[0], out[1], out[2:]


def grad_b_kernel(places, scale, codes_ref, *refs):
    out_ref, total = refs[-1], None
    for (step, start), piece in zip(places, refs):
        term = jnp.dot(
            codes_ref[step, :, start : start + piece.shape[0]], piece[...],
            preferred_element_type=jnp.float32,
        )
        total = term if total is None else total + term
    out_ref[...] = total * scale


def grad_b_of(grad_codes, pieces, places, scale):
    share, columns = grad_codes.shape[1], pieces[0].shape[1]
    width = 512 if columns % 512 == 0 else 256
    tokens = sum(piece.shape[0] for piece in pieces)
    return pl.pallas_call(
        functools.partial(grad_b_kernel, places, scale),
        grid=(columns // width,),
        out_shape=jax.ShapeDtypeStruct((share, columns), jnp.float32),
        in_specs=[pl.BlockSpec(grad_codes.shape, lambda i: (0, 0, 0))]
        + [pl.BlockSpec((piece.shape[0], width), lambda i: (0, i)) for piece in pieces],
        out_specs=pl.BlockSpec((share, width), lambda i: (0, i)),
        compiler_params=pltpu.CompilerParams(vmem_limit_bytes=48 * 2**20),
        cost_estimate=pl.CostEstimate(
            flops=2 * share * columns * tokens,
            bytes_accessed=columns * (2 * tokens + 4 * share),
            transcendentals=0,
        ),
    )(grad_codes, *pieces)


def gather_start(acts, toks):
    if toks != 4:
        return [lax.all_gather(acts, "tok", axis=0, tiled=False)]
    return [
        lax.ppermute(acts, "tok", [(t, t ^ step) for t in range(toks)]) for step in (1, 2)
    ]


def gather_end(acts, begun, toks, tok):
    tokens = acts.shape[0]
    if toks != 4:
        (whole,) = begun
        pieces = [acts] + [
            lax.dynamic_index_in_dim(whole, tok ^ step, 0, keepdims=False)
            for step in range(1, toks)
        ]
        return [(step, 0) for step in range(toks)], pieces

    def move(x, step):
        return lax.ppermute(x, "tok", [(t, t ^ step) for t in range(toks)])

    half = tokens // 2
    along_x, along_y = begun
    low, high = move(along_x[:half], 2), move(along_y[half:], 1)
    return [(0, 0), (1, 0), (2, 0), (3, 0), (3, half)], [acts, along_x, along_y, low, high]


def local(acts, target, proj_b, proj_a):
    toks, chans = lax.axis_size("tok"), lax.axis_size("chan")
    tok = lax.axis_index("tok")
    tokens, rank = acts.shape[0], proj_b.shape[0]
    factor_scale = -2.0 / (tokens * toks)
    begun = gather_start(acts, toks)

    codes_part = lax.dot_general(
        proj_b, acts, (((1,), (1,)), ((), ())), preferred_element_type=jnp.float32
    )
    codes = sum_codes(codes_part, chans)
    codes, begun = lax.optimization_barrier((codes, begun))
    places, pieces = gather_end(acts, begun, toks, tok)
    piece, own, terms = grads(codes, proj_a, target, chans, toks)

    def move(x, step):
        return lax.ppermute(x, "tok", [(t, t ^ step) for t in range(toks)])

    if toks == 4:
        from_x, from_y = move(terms[0], 1), move(terms[1], 2)
    else:
        first = [move(value, step + 1) for step, value in enumerate(terms)]
    grad_codes = gather_codes(piece, chans)
    if toks == 4:
        grad_codes, from_x, from_y = lax.optimization_barrier((grad_codes, from_x, from_y))
        to_y = terms[2][0].astype(jnp.float32) + from_x[1].astype(jnp.float32)
        to_x = terms[2][1].astype(jnp.float32) + from_y[1].astype(jnp.float32)
        low, high = move(to_y.astype(jnp.bfloat16), 2), move(to_x.astype(jnp.bfloat16), 1)
        grad_b = grad_b_of(grad_codes, pieces, places, factor_scale)
        grad_b, low, high = lax.optimization_barrier((grad_b, low, high))
        low, high = low.astype(jnp.float32), high.astype(jnp.float32)
        grad_a = own + jnp.concatenate(
            [from_x[0].astype(jnp.float32) + low, from_y[0].astype(jnp.float32) + high]
        )
    else:
        grad_a = own + sum(value.reshape(own.shape).astype(jnp.float32) for value in first)
        grad_b = grad_b_of(grad_codes, pieces, places, factor_scale)
    return (grad_a * factor_scale, grad_b)


def solution(mesh):
    return jax.shard_map(
        local,
        mesh=mesh,
        in_specs=(P("tok", "chan"), P("tok", "chan"), P(None, "chan"), P("chan", None)),
        out_specs=(P("chan", "tok"), P("tok", "chan")),
        check_vma=False,
    )
```

time: 504 us -> 178 us (0.35)
  waiting for transfers between devices: 252 us -> 12.1 us
  blocking collectives: 178 us -> 0 us
  Pallas kernels: 0 us -> 135 us
  matrix products: 46 us -> 13.4 us
  between operations: 14.1 us -> 0.72 us
  starting transfers between devices: 0.08 us -> 11.7 us
  other arithmetic: 9.86 us -> 2.43 us
    reduce_scatter x2 -> x0, waiting for transfers between devices: 252 us -> none  [the longest x1 252 us: local(): lax.psum_scatter(contract_rows(grad_codes, acts), 'tok', scatter_dimensio...]
    psum x2 -> x0, blocking collectives: 178 us -> none  [the longest x1 90.8 us: local(): codes = lax.psum(partial_value, 'chan').astype(jnp.bfloat16)]
    pallas_call x0 -> x4, Pallas kernels: none -> 135 us  [the longest x3 122 us: call(): pl.pallas_call(kernel, out_shape=out_shape, in_specs=[vmem] * len(operand...]
    dot_general x5 -> x1, matrix products: 46 us -> 13.4 us  [local(): lax.dot_general(proj_b, acts, (((1,), (1,)), ((), ())), preferred_element...]
    ppermute x0 -> x8, waiting for transfers between devices: none -> 12.1 us  [the longest x2 11.4 us: gather_start(): lax.ppermute(acts, 'tok', [(t, t ^ step) for t in range(toks)])]
    ppermute x0 -> x8, starting transfers between devices: none -> 11.7 us  [the longest x6 7.16 us: move(): return lax.ppermute(x, 'tok', [(t, t ^ step) for t in range(toks)])]
    mul x2 -> x1, other arithmetic: 9.86 us -> 1.82 us  [local(): return (grad_a * factor_scale, grad_b)]
  transfers between devices with their start and end apart: 2 -> 8, of which waited for: 1 -> 3; matrix products, arithmetic and copies ran while one was open for 5% -> 8% of each run, Pallas kernels for 0% -> 76%
where the time goes in v3:
time: 178 us
  Pallas kernels  135 us (76%)
  matrix products  13.4 us (8%)
  waiting for transfers between devices  12.1 us (7%)
  starting transfers between devices  11.7 us (7%)
  local copies, waits for them, and re-layouts  2.54 us (1%)
  other arithmetic  2.43 us (1%)
    pallas_call x3, Pallas kernels, call(): pl.pallas_call(kernel, out_shape=out_shape, in_specs=[vmem] * len(operand...  122 us
    dot_general x1, matrix products, local(): lax.dot_general(proj_b, acts, (((1,), (1,)), ((), ())), preferred_element...  13.4 us
    pallas_call x1, Pallas kernels, grad_b_of(): pl.pallas_call(functools.partial(grad_b_kernel, places, scale), grid=(col...  12.7 us
    ppermute x2, waiting for transfers between devices, gather_start(): lax.ppermute(acts, 'tok', [(t, t ^ step) for t in range(toks)])  11.4 us
    ppermute x6, starting transfers between devices, move(): return lax.ppermute(x, 'tok', [(t, t ^ step) for t in range(toks)])  7.16 us
    ppermute x2, starting transfers between devices, gather_start(): lax.ppermute(acts, 'tok', [(t, t ^ step) for t in range(toks)])  4.52 us
  transfers between devices with their start and end apart: 8, of which 3 were waited for; matrix products, arithmetic and copies ran while one was open for 8% of the time, Pallas kernels for 76%

profile of v3, /device:TPU:0, one launch (start us, length us, event | category | flops | bytes accessed | tf_op | source)
XLA Modules:
  0.0 178.0 jit_solution(5532370147360468733)
XLA Ops:
  0.6 3.0 %collective-permute-start = (bf16[512,3584]{1,0:T(8,128)(2,1)}, bf16[512,3584]{1,0:T(8,128)(2,1)S(1)}, u32[]{:S(2)}, u32[]{:S(2)}) collective-permute-start(bf16[512,3584]{1,0:T(8,128)(2,1)} %refs_0_.1), channel_id=1, source_target_pairs={{0,8},{8,0},{16,24},{24,16},{1,9},{9,1},{17,25},{25,17},{2,10},{10... | collective-permute-start | bytes 11010056 | tf_op jit(solution)/shard_map/ppermute | solution.py:342
  3.6 1.5 collective-permute-start.1
  5.2 13.4 %fusion.3 = f32[2048,512]{1,0:T(8,128)} fusion(bf16[2048,3584]{1,0:T(8,128)(2,1)} %param.6, bf16[512,3584]{1,0:T(8,128)(2,1)} %refs_0_.1), kind=kOutput, calls=%fused_computation.8 | convolution fusion | flops 7516192768 | bytes 22544384 | tf_op jit(solution)/shard_map/dot_general | solution.py:372
  18.6 54.7 %shard_map.59 = bf16[1,2,4,256,512]{4,3,2,1,0:T(8,128)(2,1)S(1)} custom-call(f32[1,2,4,256,512]{4,3,2,1,0:T(8,128)} %bitcast.17), custom_call_target="tpu_custom_call" | custom-call | bytes 1024 | tf_op jit(solution)/shard_map/pallas_call | solution.py:236
  73.3 0.0 copy-start
  73.3 9.9 %collective-permute-done.refs_1_ = bf16[512,3584]{1,0:T(8,128)(2,1)S(1)} collective-permute-done((bf16[512,3584]{1,0:T(8,128)(2,1)}, bf16[512,3584]{1,0:T(8,128)(2,1)S(1)}, u32[]{:S(2)}, u32[]{:S(2)}) %collective-permute-start) | collective-permute-done | bytes 3670048 | tf_op jit(solution)/shard_map/ppermute | solution.py:342
  83.2 0.0 copy-start.3
  83.2 1.5 collective-permute-done.1.refs_2_
  84.6 0.0 copy-start.4
  84.6 0.3 copy-done.3
  85.0 0.1 slice.25
  85.1 1.4 copy-done.4
  86.5 0.0 copy-start.1
  86.5 0.1 slice.26
  86.6 0.0 copy-done
  86.6 1.4 collective-permute-start.5
  88.1 1.5 collective-permute-start.4
  89.6 0.0 copy-done.1
  89.6 43.5 %shard_map.60 = (bf16[4,64,512]{2,1,0:T(8,128)(2,1)S(1)}, f32[1024,512]{1,0:T(8,128)}, bf16[2,512,512]{2,1,0:T(8,128)(2,1)S(1)}, bf16[2,512,512]{2,1,0:T(8,128)(2,1)S(1)}, bf16[2,512,512]{2,1,0:T(8,128)(2,1)S(1)}) custom-call(bf16[2048,512]{1,0:T(8,128)(2,1)} %bitcast.15, bf16[1024,2048]{1,0:T(8,128)(2,1)} %a_ref.1, bf16[512,1024]{1,0:T(8,128)(2,1)S(1)} %copy-done.1), custom_call_target="tpu_custom_call" | custom-call | bytes 1024 | tf_op jit(solution)/shard_map/pallas_call | solution.py:236
  133.1 1.3 collective-permute-start.2
  134.4 0.8 collective-permute-start.3
  135.2 24.3 %shard_map.61 = bf16[4,2,4,64,512]{4,3,2,1,0:T(8,128)(2,1)S(1)} custom-call(bf16[4,64,512]{2,1,0:T(8,128)(2,1)S(1)} %get-tuple-element.18.piece_ref), custom_call_target="tpu_custom_call" | custom-call | bytes 1024 | tf_op jit(solution)/shard_map/pallas_call | solution.py:236
  159.5 0.0 collective-permute-done.2
  159.5 0.0 collective-permute-done.3
  159.5 0.3 fusion.2
  159.8 1.6 collective-permute-start.7
  161.4 0.5 collective-permute-start.6
  161.9 0.0 collective-permute-done.5.refs_4_
  161.9 0.0 collective-permute-done.4.refs_3_
  161.9 12.7 %shard_map.62 = f32[512,3584]{1,0:T(8,128)} custom-call(bf16[4,512,512]{2,1,0:T(8,128)(2,1)S(1)} %bitcast.16, bf16[512,3584]{1,0:T(8,128)(2,1)} %refs_0_.1, bf16[512,3584]{1,0:T(8,128)(2,1)} %copy-done.3, bf16[512,3584]{1,0:T(8,128)(2,1)} %copy-done.4, bf16[256,3584]{1,0:T(8,128)(2,1)S(1)} %collective-permute-done.4.refs_3_, ...), custom_call_target="tpu_custom_call" | custom-call | flops 7516192768 | bytes 22020096 | tf_op jit(solution)/shard_map/pallas_call | solution.py:322
  174.6 0.0 copy-start.2
  174.6 0.0 collective-permute-done.7
  174.6 0.7 collective-permute-done.6
  175.3 0.3 convert_add_fusion
  175.6 0.6 copy-done.2
  176.2 1.8 %fusion = f32[1024,512]{1,0:T(8,128)} fusion(f32[1024,512]{1,0:T(8,128)S(1)} %copy-done.2, f32[512,512]{1,0:T(8,128)S(1)} %get-tuple-element.32, f32[512,512]{1,0:T(8,128)S(1)} %get-tuple-element.33), kind=kLoop, calls=%fused_computation.1 | loop fusion | flops 1572864 | bytes 6291456 | tf_op jit(solution)/shard_map/mul | solution.py:402
Async XLA Ops:
  0.6 82.6 %collective-permute-start = (bf16[512,3584]{1,0:T(8,128)(2,1)}, bf16[512,3584]{1,0:T(8,128)(2,1)S(1)}, u32[]{:S(2)}, u32[]{:S(2)}) collective-permute-start(bf16[512,3584]{1,0:T(8,128)(2,1)} %refs_0_.1), channel_id=1, source_target_pairs={{0,8},{8,0},{16,24},{24,16},{1,9},{9,1},{17,25},{25,17},{2,10},{10... | collective-permute-start | bytes 11010056 | tf_op jit(solution)/shard_map/ppermute | solution.py:342
  3.6 81.0 %collective-permute-start.1 = (bf16[512,3584]{1,0:T(8,128)(2,1)}, bf16[512,3584]{1,0:T(8,128)(2,1)S(1)}, u32[]{:S(2)}, u32[]{:S(2)}) collective-permute-start(bf16[512,3584]{1,0:T(8,128)(2,1)} %refs_0_.1), channel_id=1, source_target_pairs={{0,16},{8,24},{16,0},{24,8},{1,17},{9,25},{17,1},{25,9},{2,18},{10... | collective-permute-start | bytes 11010056 | tf_op jit(solution)/shard_map/ppermute | solution.py:342
  73.3 13.3 %copy-start = (bf16[1,2,4,256,512]{4,3,2,1,0:T(8,128)(2,1)}, bf16[1,2,4,256,512]{4,3,2,1,0:T(8,128)(2,1)S(1)}, u32[]{:S(2)}) copy-start(bf16[1,2,4,256,512]{4,3,2,1,0:T(8,128)(2,1)S(1)} %shard_map.59) | copy-start | bytes 6291460
  83.2 1.8 %copy-start.3 = (bf16[512,3584]{1,0:T(8,128)(2,1)}, bf16[512,3584]{1,0:T(8,128)(2,1)S(1)}, u32[]{:S(2)}) copy-start(bf16[512,3584]{1,0:T(8,128)(2,1)S(1)} %collective-permute-done.refs_1_) | copy-start | bytes 11010052
  84.6 1.8 %copy-start.4 = (bf16[512,3584]{1,0:T(8,128)(2,1)}, bf16[512,3584]{1,0:T(8,128)(2,1)S(1)}, u32[]{:S(2)}) copy-start(bf16[512,3584]{1,0:T(8,128)(2,1)S(1)} %collective-permute-done.1.refs_2_) | copy-start | bytes 11010052
  86.5 3.1 %copy-start.1 = (bf16[512,1024]{1,0:T(8,128)(2,1)S(1)}, bf16[512,1024]{1,0:T(8,128)(2,1)}, u32[]{:S(2)}) copy-start(bf16[512,1024]{1,0:T(8,128)(2,1)} %target_ref.1) | copy-start | bytes 3145732
  86.6 75.3 %collective-permute-start.5 = (bf16[256,3584]{1,0:T(8,128)(2,1)S(1)}, bf16[256,3584]{1,0:T(8,128)(2,1)S(1)}, u32[]{:S(2)}, u32[]{:S(2)}) collective-permute-start(bf16[256,3584]{1,0:T(8,128)(2,1)S(1)} %slice.26), channel_id=1, source_target_pairs={{0,8},{8,0},{16,24},{24,16},{1,9},{9,1},{17,25},{25,17},{2,10},{10... | collective-permute-start | bytes 5505032 | tf_op jit(solution)/shard_map/ppermute | solution.py:357
  88.1 73.8 %collective-permute-start.4 = (bf16[256,3584]{1,0:T(8,128)(2,1)S(1)}, bf16[256,3584]{1,0:T(8,128)(2,1)S(1)}, u32[]{:S(2)}, u32[]{:S(2)}) collective-permute-start(bf16[256,3584]{1,0:T(8,128)(2,1)S(1)} %slice.25), channel_id=1, source_target_pairs={{0,16},{8,24},{16,0},{24,8},{1,17},{9,25},{17,1},{25,9},{2,18},{10... | collective-permute-start | bytes 5505032 | tf_op jit(solution)/shard_map/ppermute | solution.py:357
  133.1 26.4 %collective-permute-start.2 = (bf16[2,512,512]{2,1,0:T(8,128)(2,1)S(1)}, bf16[2,512,512]{2,1,0:T(8,128)(2,1)S(1)}, u32[]{:S(2)}, u32[]{:S(2)}) collective-permute-start(bf16[2,512,512]{2,1,0:T(8,128)(2,1)S(1)} %get-tuple-element.19), channel_id=1, source_target_pairs={{0,8},{8,0},{16,24},{24,16},{1,9},{9,1},{17,25},{25,17},{2,10},{10... | collective-permute-start | bytes 3145736 | tf_op jit(solution)/shard_map/ppermute | solution.py:381
  134.4 25.1 %collective-permute-start.3 = (bf16[2,512,512]{2,1,0:T(8,128)(2,1)S(1)}, bf16[2,512,512]{2,1,0:T(8,128)(2,1)S(1)}, u32[]{:S(2)}, u32[]{:S(2)}) collective-permute-start(bf16[2,512,512]{2,1,0:T(8,128)(2,1)S(1)} %get-tuple-element.20), channel_id=1, source_target_pairs={{0,16},{8,24},{16,0},{24,8},{1,17},{9,25},{17,1},{25,9},{2,18},{10... | collective-permute-start | bytes 3145736 | tf_op jit(solution)/shard_map/ppermute | solution.py:381
  159.8 14.8 %collective-permute-start.7 = (bf16[512,512]{1,0:T(8,128)(2,1)S(1)}, bf16[512,512]{1,0:T(8,128)(2,1)S(1)}, u32[]{:S(2)}, u32[]{:S(2)}) collective-permute-start(bf16[512,512]{1,0:T(8,128)(2,1)S(1)} %get-tuple-element.30), channel_id=1, source_target_pairs={{0,8},{8,0},{16,24},{24,16},{1,9},{9,1},{17,25},{25,17},{2,10},{10... | collective-permute-start | bytes 1572872 | tf_op jit(solution)/shard_map/ppermute | solution.py:381
  161.4 13.9 %collective-permute-start.6 = (bf16[512,512]{1,0:T(8,128)(2,1)S(1)}, bf16[512,512]{1,0:T(8,128)(2,1)S(1)}, u32[]{:S(2)}, u32[]{:S(2)}) collective-permute-start(bf16[512,512]{1,0:T(8,128)(2,1)S(1)} %get-tuple-element.31), channel_id=1, source_target_pairs={{0,16},{8,24},{16,0},{24,8},{1,17},{9,25},{17,1},{25,9},{2,18},{10... | collective-permute-start | bytes 1572872 | tf_op jit(solution)/shard_map/ppermute | solution.py:381
  174.6 1.6 copy-start.2

commit v4 on v3

--- a/solution.py
+++ b/solution.py
@@ -335,16 +335,27 @@
     )(grad_codes, *pieces)
 
 
+def move(x, step):
+    toks = lax.axis_size("tok")
+    return lax.ppermute(x, "tok", [(t, t ^ step) for t in range(toks)])
+
+
 def gather_start(acts, toks):
     if toks != 4:
         return [lax.all_gather(acts, "tok", axis=0, tiled=False)]
-    return [
-        lax.ppermute(acts, "tok", [(t, t ^ step) for t in range(toks)]) for step in (1, 2)
-    ]
-
-
-def gather_end(acts, begun, toks, tok):
-    tokens = acts.shape[0]
+    half = acts.shape[0] // 2
+    return [move(acts[:half], 1), move(acts[half:], 2)]
+
+
+def gather_next(acts, toks):
+    if toks != 4:
+        return []
+    half = acts.shape[0] // 2
+    return [move(acts[half:], 1), move(acts[:half], 2)]
+
+
+def gather_end(acts, begun, rest, toks, tok):
+    half = acts.shape[0] // 2
     if toks != 4:
         (whole,) = begun
         pieces = [acts] + [
@@ -352,14 +363,10 @@
             for step in range(1, toks)
         ]
         return [(step, 0) for step in range(toks)], pieces
-
-    def move(x, step):
-        return lax.ppermute(x, "tok", [(t, t ^ step) for t in range(toks)])
-
-    half = tokens // 2
-    along_x, along_y = begun
-    low, high = move(along_x[:half], 2), move(along_y[half:], 1)
-    return [(0, 0), (1, 0), (2, 0), (3, 0), (3, half)], [acts, along_x, along_y, low, high]
+    x_low, y_high = begun
+    x_high, y_low = rest
+    places = [(0, 0), (1, 0), (1, half), (2, 0), (2, half), (3, 0), (3, half)]
+    return places, [acts, x_low, x_high, y_low, y_high, move(x_low, 2), move(y_high, 1)]
 
 
 def local(acts, target, proj_b, proj_a):
@@ -372,18 +379,19 @@
     codes_part = lax.dot_general(
         proj_b, acts, (((1,), (1,)), ((), ())), preferred_element_type=jnp.float32
     )
+    late, codes_part = lax.optimization_barrier((acts, codes_part))
+    rest = gather_next(late, toks)
     codes = sum_codes(codes_part, chans)
     codes, begun = lax.optimization_barrier((codes, begun))
-    places, pieces = gather_end(acts, begun, toks, tok)
+    places, pieces = gather_end(acts, begun, rest, toks, tok)
     piece, own, terms = grads(codes, proj_a, target, chans, toks)
-
-    def move(x, step):
-        return lax.ppermute(x, "tok", [(t, t ^ step) for t in range(toks)])
 
     if toks == 4:
         from_x, from_y = move(terms[0], 1), move(terms[1], 2)
     else:
         first = [move(value, step + 1) for step, value in enumerate(terms)]
+    if toks == 4:
+        piece, pieces[2], pieces[3] = lax.optimization_barrier((piece, pieces[2], pieces[3]))
     grad_codes = gather_codes(piece, chans)
     if toks == 4:
         grad_codes, from_x, from_y = lax.optimization_barrier((grad_codes, from_x, from_y))

time: 178 us -> 179 us (level)
  waiting for transfers between devices: 12.1 us -> 0.35 us
  local copies, waits for them, and re-layouts: 2.54 us -> 9.38 us
  Pallas kernels: 135 us -> 141 us
    ppermute x2 -> x0, waiting for transfers between devices: 11.4 us -> none  [gather_start(): lax.ppermute(acts, 'tok', [(t, t ^ step) for t in range(toks)])]
    slice x2, local copies, waits for them, and re-layouts: 0.24 us -> 5.8 us  [the longest x1 3.69 us: gather_start(): return [move(acts[:half], 1), move(acts[half:], 2)]]
    ppermute x6 -> x10, starting transfers between devices: 7.16 us -> 12.5 us  [move(): return lax.ppermute(x, 'tok', [(t, t ^ step) for t in range(toks)])]
    pallas_call x3, Pallas kernels: 122 us -> 128 us  [call(): pl.pallas_call(kernel, out_shape=out_shape, in_specs=[vmem] * len(operand...]
    ppermute x2 -> x0, starting transfers between devices: 4.52 us -> none  [gather_start(): lax.ppermute(acts, 'tok', [(t, t ^ step) for t in range(toks)])]
  transfers between devices with their start and end apart: 8 -> 10, of which waited for: 3 -> 2; matrix products, arithmetic and copies ran while one was open for 8% -> 8% of each run, Pallas kernels for 76% -> 79%
where the time goes in v4:
time: 179 us
  Pallas kernels  141 us (79%)
  starting transfers between devices  12.5 us (7%)
  matrix products  12.4 us (7%)
  local copies, waits for them, and re-layouts  9.38 us (5%)
  other arithmetic  2.41 us (1%)
    pallas_call x3, Pallas kernels, call(): pl.pallas_call(kernel, out_shape=out_shape, in_specs=[vmem] * len(operand...  128 us
    pallas_call x1, Pallas kernels, grad_b_of(): pl.pallas_call(functools.partial(grad_b_kernel, places, scale), grid=(col...  13.1 us
    ppermute x10, starting transfers between devices, move(): return lax.ppermute(x, 'tok', [(t, t ^ step) for t in range(toks)])  12.5 us
    dot_general x1, matrix products, local(): lax.dot_general(proj_b, acts, (((1,), (1,)), ((), ())), preferred_element...  12.4 us
    slice x1, local copies, waits for them, and re-layouts, gather_start(): return [move(acts[:half], 1), move(acts[half:], 2)]  3.69 us
  transfers between devices with their start and end apart: 10, of which 2 were waited for; matrix products, arithmetic and copies ran while one was open for 8% of the time, Pallas kernels for 79%

profile of v4, /device:TPU:0, one launch (start us, length us, event | category | flops | bytes accessed | tf_op | source)
XLA Modules:
  0.0 178.5 jit_solution(7531922817408472751)
XLA Ops:
  0.6 0.0 copy-start.3
  0.6 3.7 %fusion.4 = (bf16[256,3584]{1,0:T(8,128)(2,1)}, bf16[256,3584]{1,0:T(8,128)(2,1)S(1)}) fusion(bf16[512,3584]{1,0:T(8,128)(2,1)} %refs_0_.1), kind=kLoop, calls=%fused_computation.9 | loop fusion | bytes 7340032 | tf_op jit(solution)/shard_map/slice | solution.py:347
  4.3 3.0 %collective-permute-start.1 = (bf16[256,3584]{1,0:T(8,128)(2,1)}, bf16[256,3584]{1,0:T(8,128)(2,1)S(1)}, u32[]{:S(2)}, u32[]{:S(2)}) collective-permute-start(bf16[256,3584]{1,0:T(8,128)(2,1)} %get-tuple-element.42), channel_id=1, source_target_pairs={{0,16},{8,24},{16,0},{24,8},{1,17},{9,25},{17,1},{25,9},{2,18},{10... | collective-permute-start | bytes 5505032 | tf_op jit(solution)/shard_map/ppermute | solution.py:340
  7.3 1.5 collective-permute-start
  8.8 0.0 copy-done.3
  8.8 12.4 %fusion.5 = f32[2048,512]{1,0:T(8,128)} fusion(bf16[2048,3584]{1,0:T(8,128)(2,1)} %param.6, bf16[512,3584]{1,0:T(8,128)(2,1)S(1)} %copy-done.3), kind=kOutput, calls=%fused_computation.10 | convolution fusion | flops 7516192768 | bytes 22544384 | tf_op jit(solution)/shard_map/dot_general | solution.py:379
  21.1 2.1 %fusion.3 = (bf16[256,3584]{1,0:T(8,128)(2,1)}, bf16[256,3584]{1,0:T(8,128)(2,1)}) fusion(bf16[512,3584]{1,0:T(8,128)(2,1)S(1)} %copy-done.3), kind=kLoop, calls=%fused_computation.8 | loop fusion | bytes 7340032 | tf_op jit(solution)/shard_map/slice | solution.py:354
  23.3 0.5 collective-permute-start.3
  23.8 0.0 collective-permute-start.2
  23.8 0.0 copy-start.2
  23.8 55.4 %shard_map.59 = bf16[1,2,4,256,512]{4,3,2,1,0:T(8,128)(2,1)S(1)} custom-call(f32[1,2,4,256,512]{4,3,2,1,0:T(8,128)} %bitcast.17), custom_call_target="tpu_custom_call" | custom-call | bytes 1024 | tf_op jit(solution)/shard_map/pallas_call | solution.py:236
  79.2 0.0 copy-start
  79.2 1.3 copy-done
  80.5 0.0 collective-permute-done.1.refs_4_
  80.5 0.0 copy-start.5
  80.5 0.0 collective-permute-done.refs_1_
  80.5 1.6 collective-permute-start.6
  82.1 1.5 collective-permute-start.7
  83.6 0.0 copy-done.2
  83.6 47.9 %shard_map.60 = (bf16[4,64,512]{2,1,0:T(8,128)(2,1)S(1)}, f32[1024,512]{1,0:T(8,128)}, bf16[2,512,512]{2,1,0:T(8,128)(2,1)S(1)}, bf16[2,512,512]{2,1,0:T(8,128)(2,1)S(1)}, bf16[2,512,512]{2,1,0:T(8,128)(2,1)S(1)}) custom-call(bf16[2048,512]{1,0:T(8,128)(2,1)} %bitcast.15, bf16[1024,2048]{1,0:T(8,128)(2,1)} %a_ref.1, bf16[512,1024]{1,0:T(8,128)(2,1)S(1)} %copy-done.2), custom_call_target="tpu_custom_call" | custom-call | bytes 1024 | tf_op jit(solution)/shard_map/pallas_call | solution.py:236
  131.5 0.0 copy-done.5
  131.5 1.8 collective-permute-start.4
  133.3 0.0 collective-permute-done.3.refs_3_
  133.3 1.5 collective-permute-start.5
  134.8 0.0 collective-permute-done.2.refs_2_
  134.8 24.5 %shard_map.61 = bf16[4,2,4,64,512]{4,3,2,1,0:T(8,128)(2,1)S(1)} custom-call(bf16[4,64,512]{2,1,0:T(8,128)(2,1)S(1)} %get-tuple-element.26.piece_ref), custom_call_target="tpu_custom_call" | custom-call | bytes 1024 | tf_op jit(solution)/shard_map/pallas_call | solution.py:236
  159.3 0.0 copy-start.1
  159.3 1.3 copy-done.1
  160.6 0.0 collective-permute-done.4
  160.6 0.0 collective-permute-done.5
  160.6 0.3 fusion.2
  160.9 0.6 collective-permute-start.9
  161.6 0.5 collective-permute-start.8
  162.1 0.0 collective-permute-done.6.refs_5_
  162.1 0.0 collective-permute-done.7.refs_6_
  162.1 13.1 %shard_map.62 = f32[512,3584]{1,0:T(8,128)} custom-call(bf16[4,512,512]{2,1,0:T(8,128)(2,1)} %bitcast.16, bf16[512,3584]{1,0:T(8,128)(2,1)} %refs_0_.1, bf16[256,3584]{1,0:T(8,128)(2,1)S(1)} %collective-permute-done.refs_1_, bf16[256,3584]{1,0:T(8,128)(2,1)S(1)} %collective-permute-done.2.refs_2_, bf16[256,3584]{1,0:T(8,128)(2,1)S(1)} %collective-permute-done.3.refs_3_, ...), custom_call_target="tpu_custom_call" | custom-call | flops 7516192768 | bytes 22020096 | tf_op jit(solution)/shard_map/pallas_call | solution.py:322
  175.1 0.0 copy-start.4
  175.1 0.1 collective-permute-done.9
  175.2 0.3 collective-permute-done.8
  175.5 0.3 convert_add_fusion
  175.8 0.9 copy-done.4
  176.7 1.8 %fusion = f32[1024,512]{1,0:T(8,128)} fusion(f32[1024,512]{1,0:T(8,128)S(1)} %copy-done.4, f32[512,512]{1,0:T(8,128)S(1)} %get-tuple-element.46, f32[512,512]{1,0:T(8,128)S(1)} %get-tuple-element.47), kind=kLoop, calls=%fused_computation.1 | loop fusion | flops 1572864 | bytes 6291456 | tf_op jit(solution)/shard_map/mul | solution.py:410
Async XLA Ops:
  0.6 8.2 %copy-start.3 = (bf16[512,3584]{1,0:T(8,128)(2,1)S(1)}, bf16[512,3584]{1,0:T(8,128)(2,1)}, u32[]{:S(2)}) copy-start(bf16[512,3584]{1,0:T(8,128)(2,1)} %refs_0_.1) | copy-start | bytes 11010052
  4.3 76.2 %collective-permute-start.1 = (bf16[256,3584]{1,0:T(8,128)(2,1)}, bf16[256,3584]{1,0:T(8,128)(2,1)S(1)}, u32[]{:S(2)}, u32[]{:S(2)}) collective-permute-start(bf16[256,3584]{1,0:T(8,128)(2,1)} %get-tuple-element.42), channel_id=1, source_target_pairs={{0,16},{8,24},{16,0},{24,8},{1,17},{9,25},{17,1},{25,9},{2,18},{10... | collective-permute-start | bytes 5505032 | tf_op jit(solution)/shard_map/ppermute | solution.py:340
  7.3 73.2 %collective-permute-start = (bf16[256,3584]{1,0:T(8,128)(2,1)S(1)}, bf16[256,3584]{1,0:T(8,128)(2,1)S(1)}, u32[]{:S(2)}, u32[]{:S(2)}) collective-permute-start(bf16[256,3584]{1,0:T(8,128)(2,1)S(1)} %get-tuple-element.43), channel_id=1, source_target_pairs={{0,8},{8,0},{16,24},{24,16},{1,9},{9,1},{17,25},{25,17},{2,10},{10... | collective-permute-start | bytes 5505032 | tf_op jit(solution)/shard_map/ppermute | solution.py:340
  23.3 110.0 %collective-permute-start.3 = (bf16[256,3584]{1,0:T(8,128)(2,1)}, bf16[256,3584]{1,0:T(8,128)(2,1)S(1)}, u32[]{:S(2)}, u32[]{:S(2)}) collective-permute-start(bf16[256,3584]{1,0:T(8,128)(2,1)} %get-tuple-element.40), channel_id=1, source_target_pairs={{0,16},{8,24},{16,0},{24,8},{1,17},{9,25},{17,1},{25,9},{2,18},{10... | collective-permute-start | bytes 5505032 | tf_op jit(solution)/shard_map/ppermute | solution.py:340
  23.8 111.1 %collective-permute-start.2 = (bf16[256,3584]{1,0:T(8,128)(2,1)}, bf16[256,3584]{1,0:T(8,128)(2,1)S(1)}, u32[]{:S(2)}, u32[]{:S(2)}) collective-permute-start(bf16[256,3584]{1,0:T(8,128)(2,1)} %get-tuple-element.41), channel_id=1, source_target_pairs={{0,8},{8,0},{16,24},{24,16},{1,9},{9,1},{17,25},{25,17},{2,10},{10... | collective-permute-start | bytes 5505032 | tf_op jit(solution)/shard_map/ppermute | solution.py:340
  23.8 59.8 %copy-start.2 = (bf16[512,1024]{1,0:T(8,128)(2,1)S(1)}, bf16[512,1024]{1,0:T(8,128)(2,1)}, u32[]{:S(2)}) copy-start(bf16[512,1024]{1,0:T(8,128)(2,1)} %target_ref.1) | copy-start | bytes 3145732
  79.2 1.3 copy-start
  80.5 51.0 %copy-start.5 = (bf16[256,3584]{1,0:T(8,128)(2,1)}, bf16[256,3584]{1,0:T(8,128)(2,1)S(1)}, u32[]{:S(2)}) copy-start(bf16[256,3584]{1,0:T(8,128)(2,1)S(1)} %collective-permute-done.1.refs_4_) | copy-start | bytes 5505028
  80.5 81.5 %collective-permute-start.6 = (bf16[256,3584]{1,0:T(8,128)(2,1)S(1)}, bf16[256,3584]{1,0:T(8,128)(2,1)}, u32[]{:S(2)}, u32[]{:S(2)}) collective-permute-start(bf16[256,3584]{1,0:T(8,128)(2,1)S(1)} %collective-permute-done.refs_1_), channel_id=1, source_target_pairs={{0,16},{8,24},{16,0},{24,8},{1,17},{9,25},{17,1},{25,9},{2,18},{10... | collective-permute-start | bytes 5505032 | tf_op jit(solution)/shard_map/ppermute | solution.py:340
  82.1 79.9 %collective-permute-start.7 = (bf16[256,3584]{1,0:T(8,128)(2,1)S(1)}, bf16[256,3584]{1,0:T(8,128)(2,1)}, u32[]{:S(2)}, u32[]{:S(2)}) collective-permute-start(bf16[256,3584]{1,0:T(8,128)(2,1)S(1)} %collective-permute-done.1.refs_4_), channel_id=1, source_target_pairs={{0,8},{8,0},{16,24},{24,16},{1,9},{9,1},{17,25},{25,17},{2,10},{10... | collective-permute-start | bytes 5505032 | tf_op jit(solution)/shard_map/ppermute | solution.py:340
  131.5 29.1 %collective-permute-start.4 = (bf16[2,512,512]{2,1,0:T(8,128)(2,1)S(1)}, bf16[2,512,512]{2,1,0:T(8,128)(2,1)S(1)}, u32[]{:S(2)}, u32[]{:S(2)}) collective-permute-start(bf16[2,512,512]{2,1,0:T(8,128)(2,1)S(1)} %get-tuple-element.27), channel_id=1, source_target_pairs={{0,8},{8,0},{16,24},{24,16},{1,9},{9,1},{17,25},{25,17},{2,10},{10... | collective-permute-start | bytes 3145736 | tf_op jit(solution)/shard_map/ppermute | solution.py:340
  133.3 27.3 %collective-permute-start.5 = (bf16[2,512,512]{2,1,0:T(8,128)(2,1)S(1)}, bf16[2,512,512]{2,1,0:T(8,128)(2,1)S(1)}, u32[]{:S(2)}, u32[]{:S(2)}) collective-permute-start(bf16[2,512,512]{2,1,0:T(8,128)(2,1)S(1)} %get-tuple-element.28), channel_id=1, source_target_pairs={{0,16},{8,24},{16,0},{24,8},{1,17},{9,25},{17,1},{25,9},{2,18},{10... | collective-permute-start | bytes 3145736 | tf_op jit(solution)/shard_map/ppermute | solution.py:340
  159.3 1.3 copy-start.1
  160.9 14.3 %collective-permute-start.9 = (bf16[512,512]{1,0:T(8,128)(2,1)S(1)}, bf16[512,512]{1,0:T(8,128)(2,1)S(1)}, u32[]{:S(2)}, u32[]{:S(2)}) collective-permute-start(bf16[512,512]{1,0:T(8,128)(2,1)S(1)} %get-tuple-element.44), channel_id=1, source_target_pairs={{0,8},{8,0},{16,24},{24,16},{1,9},{9,1},{17,25},{25,17},{2,10},{10... | collective-permute-start | bytes 1572872 | tf_op jit(solution)/shard_map/ppermute | solution.py:340
  161.6 13.9 %collective-permute-start.8 = (bf16[512,512]{1,0:T(8,128)(2,1)S(1)}, bf16[512,512]{1,0:T(8,128)(2,1)S(1)}, u32[]{:S(2)}, u32[]{:S(2)}) collective-permute-start(bf16[512,512]{1,0:T(8,128)(2,1)S(1)} %get-tuple-element.45), channel_id=1, source_target_pairs={{0,16},{8,24},{16,0},{24,8},{1,17},{9,25},{17,1},{25,9},{2,18},{10... | collective-permute-start | bytes 1572872 | tf_op jit(solution)/shard_map/ppermute | solution.py:340
  175.1 1.6 copy-start.4
